TPU v7x, 256 devices: a whole 4x4x8 slice. The times are simulated.
256 devices in a mesh: grp: 16 (over y_lo, z), blk: 8 (over x, core), tp: 2 (over y_hi).
Axes of the slice: x: 4, y: 4 (y_hi: 2, y_lo: 2; y = y_hi * 2 + y_lo), z: 8, core: 2. Of those that a mesh axis runs over, the one named last changes fastest.
Arguments:
- queries: bfloat16 [2048, 4096], P('grp', ('blk', 'tp')), may hold values from -110 to 110
- keys: bfloat16 [2048, 4096], P('grp', ('blk', 'tp')), may hold values from -5 to 5
- values: bfloat16 [2048, 4096], P('grp', ('blk', 'tp')), may hold values from -6 to 6
- cross_queries: bfloat16 [2048, 4096], P('grp', ('blk', 'tp')), may hold values from -110 to 110
- history_keys: bfloat16 [3072, 4096], P('grp', ('blk', 'tp')), may hold values from -5 to 5
- history_values: bfloat16 [3072, 4096], P('grp', ('blk', 'tp')), may hold values from -6 to 6
- frame_ids: int32 [2048], replicated, may hold values from 0 to 31, never falling along the last dimension, each value on 1 to 128 neighbouring positions
- masked: int32 [2048], replicated, may hold values 0 or 1
- out_weight: bfloat16 [4096, 5120], P(('blk', 'tp')), may hold values from -0.09375 to 0.09375
- cotangent: bfloat16 [2048, 5120], P('grp', ('blk', 'tp')), may hold values from -6 to 6
Outputs:
- layer_out: bfloat16 [2048, 5120], P('grp', ('blk', 'tp'))
- query_grad: bfloat16 [2048, 4096], P('grp', ('blk', 'tp'))
- key_grad: bfloat16 [2048, 4096], P('grp', ('blk', 'tp'))
- value_grad: bfloat16 [2048, 4096], P('grp', ('blk', 'tp'))
- cross_query_grad: bfloat16 [2048, 4096], P('grp', ('blk', 'tp'))
- history_key_grad: bfloat16 [3072, 4096], P('grp', ('blk', 'tp'))
- history_value_grad: bfloat16 [3072, 4096], P('grp', ('blk', 'tp'))
- weight_grad: float32 [4096, 5120], P(('blk', 'tp'), 'grp')
Inputs may be any that keep to these rules, and one draw needn't show every extreme that they name: `frame_ids`: frame numbers never fall along the tokens; a frame holds 1 to 128 tokens.
All inputs are finite; a program needn't handle non-finite values.
Results may differ from a plain program's by a relative error of at most 0.017.
Values may be sent and summed in bfloat16 or wider, within the bound.
A program may use at most 128 MiB of HBM per device.

v0:
```python
import jax
import jax.numpy as jnp
from jax import lax
from jax.sharding import Mesh
from jax.sharding import PartitionSpec as P

HD = 128
GRP = ("grp_0", "grp_1")


def in_order(pieces, dim):
    dims = list(pieces.shape[1:])
    dims[dim] *= pieces.shape[0]
    return jnp.moveaxis(pieces, 0, dim).reshape(dims)


def gather_packed(arrays, axis, dims):
    line = jnp.concatenate([a.reshape(-1) for a in arrays])
    lines, at, done = (lax.all_gather(line, axis), 0, [])
    for a, dim in zip(arrays, dims):
        pieces = lines[:, at : at + a.size].reshape(-1, *a.shape)
        done.append(in_order(pieces, dim))
        at += a.size
    return tuple(done)


def split_up(array, dim, length):
    before, after = (array.shape[:dim], array.shape[dim + 1 :])
    return jnp.moveaxis(array.reshape(*before, length, -1, *after), dim, 0)


def summed_on_arrival(array, axis, dim):
    length = lax.axis_size(axis)
    pieces = lax.all_to_all(split_up(array, dim, length), axis, 0, 0, tiled=True)
    return jnp.sum(pieces, axis=0)


def from_everyone(array, axis):
    length = lax.axis_size(axis)
    return lax.all_to_all(
        jnp.broadcast_to(array[None], (length, *array.shape)), axis, 0, 0, tiled=True
    )


def gather_directly(array, axis, dim):
    pieces = from_everyone(array, axis)
    return in_order(pieces, dim)


def reduced_to_own(pieces, axes, turns):
    inside = pieces.shape[1:]
    pieces = pieces.reshape(*(lax.axis_size(a) for a in axes), *inside)
    pieces = jnp.moveaxis(pieces, turns, range(len(axes))).reshape(-1, *inside)
    for k in turns:
        pieces = lax.psum_scatter(pieces, axes[k], scatter_dimension=0, tiled=True)
    return pieces[0]


def scatter_axes(array, axes, turns, dim):
    length = lax.axis_size(axes)
    return reduced_to_own(split_up(array, dim, length), axes, turns)


def side_by_side(arrays, axis, dim, along):
    widths = [a.shape[along] for a in arrays]
    both = jnp.concatenate(arrays, axis=along)
    result = lax.all_gather(both, axis, axis=dim, tiled=True)
    return tuple(jnp.split(result, [sum(widths[:k]) for k in range(1, len(widths))], axis=along))


def split_heads(matrix):
    return matrix.reshape(matrix.shape[0], matrix.shape[1] // HD, HD)


def merge_heads(tensor):
    return tensor.reshape(tensor.shape[0], tensor.shape[1] * tensor.shape[2])


def visible(query_frames, key_frames, key_masked, query_index, key_index):
    causal = key_frames[None, :] <= query_frames[:, None]
    open_key = (key_masked[None, :] == 0) | (key_index[None, :] == query_index[:, None])
    return causal & open_key


def scores_of(query_split, key_split, factor):
    return (
        jnp.einsum("qhd,khd->hqk", query_split, key_split, preferred_element_type=jnp.float32)
        * factor
    )


def softmax_parts(score):
    highest = jnp.max(score, axis=-1, keepdims=True)
    weights = jnp.exp(score - highest)
    summed = jnp.sum(weights, axis=-1, keepdims=True)
    return (weights / summed, highest[..., 0] + jnp.log(summed[..., 0]))


def key_side(dscore, prob_low, query_split, grad_split, factor):
    key_part = merge_heads(
        jnp.einsum("hqk,qhd->khd", dscore, query_split, preferred_element_type=jnp.float32) * factor
    )
    value_part = merge_heads(
        jnp.einsum("hqk,qhd->khd", prob_low, grad_split, preferred_element_type=jnp.float32)
    )
    return (key_part, value_part)


def on_device(
    queries,
    keys,
    values,
    cross_queries,
    history_keys,
    history_values,
    frame_ids,
    masked,
    out_weight,
    cotangent,
):
    row_count = queries.shape[0]
    factor = HD ** (-0.5)
    row_start = lax.axis_index(GRP) * row_count
    query_index = row_start + jnp.arange(row_count, dtype=jnp.int32)
    every_key, every_value, past_keys, past_values = gather_packed(
        (keys, values, history_keys, history_values), GRP, (0, 0, 0, 0)
    )
    key_index = jnp.arange(every_key.shape[0], dtype=jnp.int32)
    query_frames = lax.dynamic_slice_in_dim(frame_ids, row_start, row_count)
    allowed = visible(query_frames, frame_ids, masked, query_index, key_index)
    query_split = split_heads(queries)
    cross_split = split_heads(cross_queries)
    key_split = split_heads(every_key)
    value_split = split_heads(every_value)
    memory_split = split_heads(past_keys)
    recall_split = split_heads(past_values)
    self_score = jnp.where(allowed[None], scores_of(query_split, key_split, factor), -jnp.inf)
    self_prob, self_log = softmax_parts(self_score)
    cross_prob, cross_log = softmax_parts(scores_of(cross_split, memory_split, factor))
    self_low = self_prob.astype(jnp.bfloat16)
    cross_low = cross_prob.astype(jnp.bfloat16)
    combined = jnp.einsum("hqk,khd->qhd", self_low, value_split, preferred_element_type=jnp.float32)
    combined = combined + jnp.einsum(
        "hqk,khd->qhd", cross_low, recall_split, preferred_element_type=jnp.float32
    )
    attended = merge_heads(combined).astype(jnp.bfloat16)
    head_terms = jnp.dot(attended, out_weight, preferred_element_type=jnp.float32)
    layer_out = summed_on_arrival(head_terms, ("blk", "tp"), 1).astype(jnp.bfloat16)
    arrived = gather_directly(cotangent, ("blk", "tp"), 1)
    grad_rows = lax.dot_general(
        arrived, out_weight, (((1,), (1,)), ((), ())), preferred_element_type=jnp.float32
    )
    product = lax.dot_general(
        attended, arrived, (((0,), (0,)), ((), ())), preferred_element_type=jnp.float32
    )
    grad_cols = product
    grad_rows, grad_cols = (grad_rows, grad_cols)
    weight_grad = scatter_axes(grad_cols.astype(jnp.bfloat16), GRP, (1, 0), 1).astype(jnp.float32)
    grad_low = grad_rows.astype(jnp.bfloat16)
    grad_split = split_heads(grad_low)
    self_dprob = jnp.einsum(
        "qhd,khd->hqk", grad_split, value_split, preferred_element_type=jnp.float32
    )
    self_dot = jnp.sum(self_prob * self_dprob, axis=-1)
    self_dscore = (self_prob * (self_dprob - self_dot[..., None])).astype(jnp.bfloat16)
    cross_dprob = jnp.einsum(
        "qhd,khd->hqk", grad_split, recall_split, preferred_element_type=jnp.float32
    )
    cross_dot = jnp.sum(cross_prob * cross_dprob, axis=-1)
    cross_dscore = (cross_prob * (cross_dprob - cross_dot[..., None])).astype(jnp.bfloat16)
    query_grad = merge_heads(
        jnp.einsum("hqk,khd->qhd", self_dscore, key_split, preferred_element_type=jnp.float32)
        * factor
    ).astype(jnp.bfloat16)
    cross_grad = merge_heads(
        jnp.einsum("hqk,khd->qhd", cross_dscore, memory_split, preferred_element_type=jnp.float32)
        * factor
    ).astype(jnp.bfloat16)
    asked, asked_cross, asked_grad = side_by_side((queries, cross_queries, grad_low), GRP, 0, 1)
    self_dots, cross_dots, self_logs, cross_logs = side_by_side(
        (self_dot, cross_dot, self_log, cross_log), GRP, 1, 0
    )
    own_masked = lax.dynamic_slice_in_dim(masked, row_start, row_count)
    allowed_own = visible(frame_ids, query_frames, own_masked, key_index, query_index)
    asked_split = split_heads(asked)
    cross_every = split_heads(asked_cross)
    grad_every = split_heads(asked_grad)
    score_own = jnp.where(
        allowed_own[None], scores_of(asked_split, split_heads(keys), factor), -jnp.inf
    )
    prob_own = jnp.exp(score_own - self_logs[..., None])
    dprob_own = jnp.einsum(
        "qhd,khd->hqk", grad_every, split_heads(values), preferred_element_type=jnp.float32
    )
    dscore_own = (prob_own * (dprob_own - self_dots[..., None])).astype(jnp.bfloat16)
    key_part, value_part = key_side(
        dscore_own, prob_own.astype(jnp.bfloat16), asked_split, grad_every, factor
    )
    prob_past = jnp.exp(
        scores_of(cross_every, split_heads(history_keys), factor) - cross_logs[..., None]
    )
    dprob_past = jnp.einsum(
        "qhd,khd->hqk", grad_every, split_heads(history_values), preferred_element_type=jnp.float32
    )
    dscore_past = (prob_past * (dprob_past - cross_dots[..., None])).astype(jnp.bfloat16)
    memory_part, recall_part = key_side(
        dscore_past, prob_past.astype(jnp.bfloat16), cross_every, grad_every, factor
    )
    key_grad = key_part.astype(jnp.bfloat16)
    value_grad = value_part.astype(jnp.bfloat16)
    history_key_grad = memory_part.astype(jnp.bfloat16)
    history_value_grad = recall_part.astype(jnp.bfloat16)
    return (
        layer_out,
        query_grad,
        key_grad,
        value_grad,
        cross_grad,
        history_key_grad,
        history_value_grad,
        weight_grad,
    )


def solution(mesh):
    finer = Mesh(
        mesh.devices.reshape(2, 8, mesh.shape["blk"], mesh.shape["tp"]),
        ("grp_0", "grp_1", "blk", "tp"),
    )
    return jax.shard_map(
        on_device,
        mesh=finer,
        in_specs=(
            P(GRP, ("blk", "tp")),
            P(GRP, ("blk", "tp")),
            P(GRP, ("blk", "tp")),
            P(GRP, ("blk", "tp")),
            P(GRP, ("blk", "tp")),
            P(GRP, ("blk", "tp")),
            P(),
            P(),
            P(("blk", "tp"), None),
            P(GRP, ("blk", "tp")),
        ),
        out_specs=(
            P(GRP, ("blk", "tp")),
            P(GRP, ("blk", "tp")),
            P(GRP, ("blk", "tp")),
            P(GRP, ("blk", "tp")),
            P(GRP, ("blk", "tp")),
            P(GRP, ("blk", "tp")),
            P(GRP, ("blk", "tp")),
            P(("blk", "tp"), GRP),
        ),
        check_vma=False,
    )
```

profile of v0, /device:TPU:8, one launch (start us, length us, event | category | flops | bytes accessed | tf_op | source)
XLA Modules:
  0.0 270.6 jit_solution(16801719822067124721)
XLA Ops:
  7.2 1.0 copy.153
  8.2 1.0 copy.152
  9.2 0.9 copy.151
  10.1 0.9 copy.150
  11.0 0.7 pad_maximum_fusion
  11.7 2.2 broadcast_in_dim.24
  14.0 6.1 %all-to-all-start.1 = ((bf16[16,128,320]{1,2,0:T(8,128)(2,1)}), bf16[16,128,320]{1,2,0:T(8,128)(2,1)S(1)}, u32[]{:S(2)}, u32[]{:S(2)}) async-start(bf16[16,128,320]{1,2,0:T(8,128)(2,1)} %broadcast_in_dim.24), calls=%async_computation.1 | async-start | bytes 2621440 | tf_op jit(solution)/shard_map/all_to_all | solution.py:40
  20.4 1.4 fusion.61
  21.8 26.6 %all-to-all-done.1 = bf16[16,128,320]{1,2,0:T(8,128)(2,1)S(1)} async-done(((bf16[16,128,320]{1,2,0:T(8,128)(2,1)}), bf16[16,128,320]{1,2,0:T(8,128)(2,1)S(1)}, u32[]{:S(2)}, u32[]{:S(2)}) %all-to-all-start.1) | async-done | bytes 1310752 | tf_op jit(solution)/shard_map/all_to_all | solution.py:40
  48.4 2.8 %convolution_convert_fusion.2 = bf16[128,256]{1,0:T(8,128)(2,1)S(1)} fusion(bf16[128,5120]{0,1:T(8,128)(2,1)S(1)} %bitcast.161, bf16[256,5120]{1,0:T(8,128)(2,1)} %param.18), kind=kOutput, calls=%fused_computation.50 | convolution fusion | flops 335577088 | bytes 3997696 | tf_op jit(solution)/shard_map/dot_general | solution.py:150
  52.0 48.6 %all-gather.6.cloned.1.call-done = bf16[2621440]{0:T(1024)(128)(2,1)} async-done(((bf16[163840]{0:T(1024)(128)(2,1)}), bf16[2621440]{0:T(1024)(128)(2,1)}) %all-gather.6.cloned.1.call-update) | async-done | bytes 5242896 | tf_op jit(solution)/shard_map/all_gather | solution.py:19
  100.5 5.4 %reshape.256 = bf16[16,163840]{1,0:T(8,128)(2,1)} reshape(bf16[2621440]{0:T(1024)(128)(2,1)} %all-gather.6.cloned.1.call-done) | data formatting | bytes 10485760 | tf_op jit(solution)/shard_map/all_gather | solution.py:19
  106.0 3.3 %fusion.99 = (bf16[16,49152]{1,0:T(8,128)(2,1)}, bf16[16,49152]{1,0:T(8,128)(2,1)S(1)}) fusion(bf16[16,163840]{1,0:T(8,128)(2,1)} %reshape.256), kind=kLoop, calls=%fused_computation.107 | loop fusion | bytes 6291456 | tf_op jit(solution)/shard_map/slice | solution.py:21
  109.2 3.1 %fusion.100 = (bf16[16,32768]{1,0:T(8,128)(2,1)}, bf16[16,32768]{1,0:T(8,128)(2,1)}) fusion(bf16[16,163840]{1,0:T(8,128)(2,1)} %reshape.256), kind=kLoop, calls=%fused_computation.108 | loop fusion | bytes 4194304 | tf_op jit(solution)/shard_map/slice | solution.py:21
  112.3 2.6 reshape_reshape_reshape.12
  114.9 2.6 reshape_reshape_reshape.13
  117.5 3.7 %copy.102 = bf16[2048,2,128]{0,2,1:T(8,128)(2,1)} copy(bf16[2048,2,128]{2,1,0:T(2,128)(2,1)} %reshape_reshape_reshape.13) | data formatting | bytes 2097152 | tf_op jit(solution)/shard_map/reshape;reshape;reshape | solution.py:72
  121.2 2.2 reshape_reshape_reshape.14
  123.4 2.4 reshape_reshape_reshape.15
  125.8 3.0 %copy.114 = bf16[3072,2,128]{0,2,1:T(8,128)(2,1)} copy(bf16[3072,2,128]{2,1,0:T(2,128)(2,1)S(1)} %reshape_reshape_reshape.15) | data formatting | bytes 3145728 | tf_op jit(solution)/shard_map/reshape;reshape;reshape | solution.py:72
  128.8 2.0 fusion.102
  131.1 0.8 fusion.103
  132.4 1.5 copy-done.11
  135.3 1.0 fusion.37
  136.4 2.4 convolution_convert_fusion
  138.8 3.0 %copy.124 = bf16[256,5120]{0,1:T(8,128)(2,1)S(1)} copy(bf16[256,5120]{1,0:T(8,128)(2,1)} %convolution_convert_fusion) | data formatting | bytes 5242880 | tf_op jit(solution)/shard_map/convert_element_type | solution.py:158
  141.8 1.8 copy.125
  144.0 1.3 copy-done.3
  145.3 2.6 copy.96
  147.8 27.3 %all-gather.4.cloned.1.call-done = bf16[2048,768]{1,0:T(8,128)(2,1)} async-done(((bf16[128,768]{1,0:T(8,128)(2,1)}), bf16[2048,768]{1,0:T(8,128)(2,1)}) %all-gather.4.cloned.1.call-update) | async-done | bytes 3145744 | tf_op jit(solution)/shard_map/all_gather | solution.py:67
  175.1 3.3 %slice_bitcast_fusion = (bf16[256,2,8,128]{3,2,1,0:T(8,128)(2,1)}, bf16[256,2,8,128]{3,2,1,0:T(8,128)(2,1)S(1)}, bf16[2048,256]{1,0:T(8,128)(2,1)S(1)}) fusion(bf16[2048,768]{1,0:T(8,128)(2,1)} %all-gather.4.cloned.1.call-done), kind=kLoop, calls=%fused_computation.58 | loop fusion | bytes 6291456
  178.4 1.4 copy.138
  179.9 4.1 %convolution_bitcast_fusion = f32[16,128,320]{1,2,0:T(8,128)} fusion(bf16[128,256,1]{0,1,2:T(8,128)(2,1)S(1)} %bitcast.175, bf16[16,320,256]{2,1,0:T(8,128)(2,1)} %bitcast.164), kind=kOutput, calls=%fused_computation.25 | convolution fusion | flops 335544320 | bytes 5308416 | tf_op jit(solution)/shard_map/dot_general | solution.py:147
  184.0 6.3 %all-to-all-start = ((f32[16,128,320]{1,2,0:T(8,128)}), f32[16,128,320]{1,2,0:T(8,128)}, u32[]{:S(2)}, u32[]{:S(2)}) async-start(f32[16,128,320]{1,2,0:T(8,128)} %convolution_bitcast_fusion), calls=%async_computation | async-start | bytes 5242880 | tf_op jit(solution)/shard_map/all_to_all | solution.py:34
  190.6 2.0 multiply_reduce_fusion.1
  193.2 2.5 multiply_reduce_fusion
  195.8 36.1 %all_gather.15 = f32[8,2048]{1,0:T(8,128)S(1)} all-gather(f32[8,128]{1,0:T(8,128)S(1)} %pad_maximum_fusion.2), channel_id=1, replica_groups=mesh['grp_0'=2,'grp_1'=8,'blk'=8,'tp'=2] {'grp_0','grp_1'}, dimensions={1}, use_global_device_ids=true | all-gather | bytes 69632 | tf_op jit(solution)/shard_map/all_gather | solution.py:67
  231.9 1.5 fusion.46
  233.4 1.0 fusion.6
  234.3 1.6 copy.126
  235.9 2.1 fusion.42
  240.0 4.4 %fusion.36 = bf16[2,128,128]{2,1,0:T(8,128)(2,1)S(1)} fusion(bf16[3072,2,128]{0,2,1:T(8,128)(2,1)} %copy.114, f32[2,128,3072]{1,2,0:T(8,128)} %get-tuple-element.50, f32[2,128]{1,0:T(2,128)S(1)} %get-tuple-element.49, f32[2,128,3072]{1,2,0:T(8,128)} %copy-done.1, f32[2,128]{1,0:T(2,128)S(1)} %fusion.2, f32[2,128]{1,0:T(2,128)S(1)} %get-tuple-element.45), kind=kOutput, calls=%fused_computation.45 | convolution fusion | flops 205324288 | bytes 7932928 | tf_op jit(solution)/shard_map/hqk,khd->qhd/dot_general | solution.py:176
  245.1 1.9 subtract_exponential_fusion
  247.0 2.5 fusion.35
  250.2 1.8 fusion.43
  252.7 2.5 reduce_sum.47
  255.2 7.2 %reduce-scatter.5.cloned.1.call-done = bf16[1,256,320]{1,2,0:T(8,128)(2,1)} async-done(((bf16[2,256,320]{1,2,0:T(8,128)(2,1)}), bf16[1,256,320]{1,2,0:T(8,128)(2,1)}) %reduce-scatter.5.cloned.1.call-update) | async-done | bytes 163856 | tf_op jit(solution)/shard_map/reduce_scatter | solution.py:55
  262.4 1.7 bitcast_convert_fusion
  (66 shorter events, 8.7 us)
Async XLA Ops:
  7.2 93.4 %all-gather.6.cloned.1.call-start = ((), (), s32[]{:S(2)}) async-start(), calls=%async_computation.7 | async-start | bytes 5570560 | tf_op jit(solution)/shard_map/all_gather | solution.py:19
  11.7 8.5 %copy-start.18 = (s32[2048]{0:T(1024)S(1)}, s32[2048]{0:T(1024)}, u32[]{:S(2)}) copy-start(s32[2048]{0:T(1024)} %param.16) | copy-start | bytes 24580
  11.7 8.6 %copy-start.19 = (s32[2048]{0:T(1024)S(1)}, s32[2048]{0:T(1024)}, u32[]{:S(2)}) copy-start(s32[2048]{0:T(1024)} %param.17) | copy-start | bytes 24580
  14.0 34.4 %all-to-all-start.1 = ((bf16[16,128,320]{1,2,0:T(8,128)(2,1)}), bf16[16,128,320]{1,2,0:T(8,128)(2,1)S(1)}, u32[]{:S(2)}, u32[]{:S(2)}) async-start(bf16[16,128,320]{1,2,0:T(8,128)(2,1)} %broadcast_in_dim.24), calls=%async_computation.1 | async-start | bytes 2621440 | tf_op jit(solution)/shard_map/all_to_all | solution.py:40
  20.1 155.0 %all-gather.4.cloned.1.call-start = ((), (), s32[]{:S(2)}) async-start(), calls=%async_computation.4 | async-start | bytes 3342336 | tf_op jit(solution)/shard_map/all_gather | solution.py:67
  20.4 30.8 %copy-start.15 = (bf16[128,256]{1,0:T(8,128)(2,1)S(1)}, bf16[128,256]{1,0:T(8,128)(2,1)}, u32[]{:S(2)}) copy-start(bf16[128,256]{1,0:T(8,128)(2,1)} %param.10) | copy-start | bytes 196612
  20.4 30.8 %copy-start.16 = (bf16[128,256]{1,0:T(8,128)(2,1)S(1)}, bf16[128,256]{1,0:T(8,128)(2,1)}, u32[]{:S(2)}) copy-start(bf16[128,256]{1,0:T(8,128)(2,1)} %param.13) | copy-start | bytes 196612
  51.9 195.1 %reduce-scatter.3.cloned.1.call-start = ((), (), s32[]{:S(2)}) async-start(), calls=%async_computation.5 | async-start | bytes 2949120 | tf_op jit(solution)/shard_map/reduce_scatter | solution.py:55
  128.8 2.3 copy-start.6
  130.8 1.6 copy-start.4
  131.9 2.7 %copy-start.1 = (f32[2,128,3072]{1,2,0:T(8,128)}, f32[2,128,3072]{1,2,0:T(8,128)S(1)}, u32[]{:S(2)}) copy-start(f32[2,128,3072]{1,2,0:T(8,128)S(1)} %get-tuple-element.46) | copy-start | bytes 9437188
  131.9 2.0 copy-start.11
  133.9 1.4 copy-start.9
  143.5 1.7 copy-start.3
  178.4 60.3 %copy-start = (bf16[256,2,8,128]{3,2,1,0:T(8,128)(2,1)}, bf16[256,2,8,128]{3,2,1,0:T(8,128)(2,1)S(1)}, u32[]{:S(2)}) copy-start(bf16[256,2,8,128]{3,2,1,0:T(8,128)(2,1)S(1)} %get-tuple-element.37) | copy-start | bytes 3145732
  184.0 6.6 %copy-start.5 = (f32[2,128,2048]{1,2,0:T(8,128)S(1)}, f32[2,128,2048]{1,2,0:T(8,128)}, u32[]{:S(2)}) copy-start(f32[2,128,2048]{1,2,0:T(8,128)} %copy-done.4) | copy-start | bytes 6291460
  184.0 68.7 %all-to-all-start = ((f32[16,128,320]{1,2,0:T(8,128)}), f32[16,128,320]{1,2,0:T(8,128)}, u32[]{:S(2)}, u32[]{:S(2)}) async-start(f32[16,128,320]{1,2,0:T(8,128)} %convolution_bitcast_fusion), calls=%async_computation | async-start | bytes 5242880 | tf_op jit(solution)/shard_map/all_to_all | solution.py:34
  190.3 72.1 %reduce-scatter.5.cloned.1.call-start = ((), (), s32[]{:S(2)}) async-start(), calls=%async_computation.6 | async-start | bytes 491520 | tf_op jit(solution)/shard_map/reduce_scatter | solution.py:55
  190.6 2.2 copy-start.2
  190.6 2.7 copy-start.10
  193.2 38.6 %copy-start.7 = (bf16[2048,2,128]{0,2,1:T(8,128)(2,1)S(1)}, bf16[2048,2,128]{0,2,1:T(8,128)(2,1)}, u32[]{:S(2)}) copy-start(bf16[2048,2,128]{0,2,1:T(8,128)(2,1)} %copy.102) | copy-start | bytes 3145732
  231.9 1.5 copy-start.8
  231.9 1.5 copy-start.17
  233.3 2.6 copy-start.14
  240.0 5.1 %copy-start.12 = (bf16[192,256]{1,0:T(8,128)(2,1)S(1)}, bf16[192,256]{1,0:T(8,128)(2,1)}, u32[]{:S(2)}) copy-start(bf16[192,256]{1,0:T(8,128)(2,1)} %param.14) | copy-start | bytes 294916
  245.1 1.9 copy-start.13
Sparse Core Ops, SparseCore 0:
  11.8 88.6 all-gather.5
  102.3 72.7 all-gather.3
  177.7 42.9 reduce-scatter.2
  247.2 15.2 reduce-scatter.4
where the time goes:
time: 274 us; the launch traced here: 271 us
  waiting for transfers between devices  110 us (40%)
  local copies, waits for them, and re-layouts  55.7 us (20%)
  blocking collectives  36.1 us (13%)
  matrix products  33.8 us (12%)
  between operations  14.1 us (5%)
  starting transfers between devices  12.8 us (5%)
  other arithmetic  8.33 us (3%)
    all_gather x1, waiting for transfers between devices, gather_packed(): lines, at, done = (lax.all_gather(line, axis), 0, [])  48.6 us
    all_gather x1, blocking collectives, side_by_side(): result = lax.all_gather(both, axis, axis=dim, tiled=True)  36.1 us
    all_gather x1, waiting for transfers between devices, side_by_side(): result = lax.all_gather(both, axis, axis=dim, tiled=True)  27.3 us
    all_to_all x1, waiting for transfers between devices, from_everyone(): lax.all_to_all(jnp.broadcast_to(array[None], (length, *array.shape)), axi...  26.6 us
    unnamed x50, local copies, waits for them, and re-layouts  17.6 us
    another operation x6, local copies, waits for them, and re-layouts, split_heads(): return matrix.reshape(matrix.shape[0], matrix.shape[1] // HD, HD)  16.5 us
    reduce_scatter x2, waiting for transfers between devices, reduced_to_own(): pieces = lax.psum_scatter(pieces, axes[k], scatter_dimension=0, tiled=True)  7.22 us
    all_to_all x1, starting transfers between devices, summed_on_arrival(): lax.all_to_all(split_up(array, dim, length), axis, 0, 0, tiled=True)  6.34 us
  transfers between devices with their start and end apart: 6, of which 4 were waited for; matrix products, arithmetic and copies ran while one was open for 32% of the time, Pallas kernels for 0%

commit v1 on v0

v1 whole, which is shorter than its diff:
```python
import itertools

import jax
import jax.numpy as jnp
from jax import lax
from jax.experimental import pallas as pl
from jax.experimental.pallas import tpu as pltpu
from jax.sharding import Mesh
from jax.sharding import PartitionSpec as P

F32, BF16 = jnp.float32, jnp.bfloat16
HD = 128
FACTOR = HD**-0.5
NZ, NX = 8, 4
HIDDEN = -1e30
NEVER = 1e9
MESH = pl.DeviceIdType.MESH
AXES = ("yl", "z", "x", "core", "yh")
GRP, COLS = ("yl", "z"), ("x", "core", "yh")

K0, V0, HK0, HV0, KV_ROWS = 0, 256, 512, 896, 1280
OUT_AT = ((0, 128), (256, 128), (512, 128), (768, 128), (1024, 192), (1408, 192))
OUT_ROWS = 1792


def dot(a, b):
    return lax.dot_general(a, b, (((1,), (0,)), ((), ())), preferred_element_type=F32)


def dot_t(a, b):
    return lax.dot_general(a, b, (((1,), (1,)), ((), ())), preferred_element_type=F32)


def kernel(
    q, k, v, cq, hk, hv, w_hbm, cot, row, col,
    out, oq, ok, ov, ocq, ohk, ohv, att_all,
    kv, qs, gr, st, self_s, cross_s, m_s, l_s, acc_s, w, cot_in, cf, part, core_in,
    mid, x_in, y_out, y_in, grad_out, att_own, att_out, ka, dqa, xo, xi,
    send_sems, recv_sems, w_sem,
):
    yl, z, x = lax.axis_index("yl"), lax.axis_index("z"), lax.axis_index("x")
    core, yh = lax.axis_index("core"), lax.axis_index("yh")
    mate_y, mate_c, mate_h = {"yl": 1 - yl}, {"core": 1 - core}, {"yh": 1 - yh}

    def at_z(d):
        return lax.rem(z + (d + NZ), NZ)

    def at_x(d):
        return lax.rem(x + (d + NX), NX)

    peers = [mate_y, mate_c, mate_h]
    peers += [{"z": at_z(d)} for d in range(1, NZ)] + [{"x": at_x(d)} for d in range(1, NX)]
    barrier = pltpu.get_barrier_semaphore()
    for peer in peers:
        pl.semaphore_signal(barrier, inc=1, device_id=peer, device_id_type=MESH)
    w_copy = pltpu.make_async_copy(w_hbm, w, w_sem.at[0])
    w_copy.start()
    pl.semaphore_wait(barrier, len(peers))

    number = itertools.count()
    started = []

    def send(src, dst, to):
        i = next(number)
        copy = pltpu.make_async_remote_copy(
            src_ref=src, dst_ref=dst, send_sem=send_sems.at[i], recv_sem=recv_sems.at[i],
            device_id=to, device_id_type=MESH,
        )
        copy.start()
        started.append(copy)
        return copy

    def lanes(i):
        return pl.ds(pl.multiple_of(i * HD, HD), HD)

    def rows(base, i, n):
        return pl.ds(pl.multiple_of(base + i * n, 16), n)

    owned = ((k, kv, K0, 128), (hk, kv, HK0, 192), (v, kv, V0, 128), (hv, kv, HV0, 192), (q, qs, 0, 128), (cq, qs, 256, 128))
    cot_copy = send(cot, cot_in, mate_h)
    swaps = [
        send(src.at[:, lanes(1 - yl)], dst.at[z, rows(base, yl, n)], mate_y)
        for src, dst, base, n in owned
    ]
    for src, dst, base, n in owned:
        dst[z, rows(base, yl, n), :] = src[:, lanes(yl)]

    def ring_step(ref, s, before):
        for copy in before:
            copy.wait_recv()
        right, left = {"z": at_z(1)}, {"z": at_z(-1)}
        from_r, from_l = at_z(-s), at_z(s)
        if s < NZ // 2 - 1:
            return [
                send(ref.at[from_r], ref.at[from_r], right),
                send(ref.at[from_l], ref.at[from_l], left),
            ]
        half = ref.shape[1] // 2
        return [
            send(ref.at[from_r, pl.ds(0, half)], ref.at[from_r, pl.ds(0, half)], right),
            send(ref.at[from_l, pl.ds(half, half)], ref.at[from_l, pl.ds(half, half)], left),
        ]

    def wait_all(copies):
        for copy in copies:
            copy.wait_recv()

    m_s[...] = jnp.full(m_s.shape, HIDDEN, F32)
    l_s[...] = jnp.zeros(l_s.shape, F32)
    acc_s[...] = jnp.zeros(acc_s.shape, F32)

    def take_in(i, s, values):
        top = m_s[i]
        new = jnp.maximum(top, jnp.max(s, axis=1, keepdims=True))
        p = jnp.exp(s - new)
        shrink = jnp.exp(top - new)
        l_s[i] = l_s[i] * shrink + jnp.sum(p, axis=1, keepdims=True)
        acc_s[i] = acc_s[i] * shrink + dot(p.astype(BF16), values)
        m_s[i] = new

    def attend(o):
        s = dot_t(qs[z, 0:256, :], kv[o, K0 : K0 + 256, :]) * FACTOR
        keep = (row[o, 1:2, :] <= col[:, 0:1]) | (row[o, 2:3, :] == col[:, 2:3])
        s = jnp.where(keep, s, HIDDEN)
        self_s[o] = s
        take_in(0, s, kv[o, V0 : V0 + 256, :])
        s = dot_t(qs[z, 256:512, :], kv[o, HK0 : HK0 + 384, :]) * FACTOR
        cross_s[o] = s
        take_in(1, s, kv[o, HV0 : HV0 + 384, :])

    def attend_both(d):
        def body(i, carry):
            attend(lax.rem(z + NZ + d * (1 - 2 * i), NZ))
            return carry

        lax.fori_loop(0, 2, body, 0)

    wait_all(swaps[0:4])
    a0 = ring_step(kv, 0, [])
    wait_all(swaps[4:6])
    b0 = ring_step(qs, 0, [])

    cot_copy.wait_recv()
    mine = x * 2 + core

    @pl.when(yh == 0)
    def _():
        cf[mine] = jnp.concatenate([cot[...], cot_in[...]], axis=1)

    @pl.when(yh == 1)
    def _():
        cf[mine] = jnp.concatenate([cot_in[...], cot[...]], axis=1)

    def slot(d):
        return at_x(d) * 2 + core

    c_right = send(cf.at[mine], cf.at[mine], {"x": at_x(1)})
    c_left = send(cf.at[mine], cf.at[mine], {"x": at_x(-1)})
    c_core = [send(cf.at[mine], cf.at[mine], mate_c)]

    attend(z)

    c_right.wait_recv()
    c_right2 = send(cf.at[slot(-1), pl.ds(0, 64)], cf.at[slot(-1), pl.ds(0, 64)], {"x": at_x(1)})
    c_core.append(send(cf.at[slot(-1)], cf.at[slot(-1)], mate_c))
    c_left.wait_recv()
    c_left2 = send(cf.at[slot(1), pl.ds(64, 64)], cf.at[slot(1), pl.ds(64, 64)], {"x": at_x(-1)})
    c_core.append(send(cf.at[slot(1)], cf.at[slot(1)], mate_c))
    a1 = ring_step(kv, 1, a0)
    attend_both(1)
    c_right2.wait_recv()
    c_left2.wait_recv()
    c_core.append(send(cf.at[slot(2)], cf.at[slot(2)], mate_c))
    a2 = ring_step(kv, 2, a1)
    b1 = ring_step(qs, 1, b0)

    wait_all(c_core)
    w_copy.wait()
    grad = dot_t(cf[0], w[:, 0:640])
    for b in range(1, 8):
        grad = grad + dot_t(cf[b], w[:, 640 * b : 640 * (b + 1)])
    grad_out[...] = grad.astype(BF16)
    g_swap = send(grad_out.at[:, lanes(1 - yl)], gr.at[z, rows(0, yl, 128)], mate_y)
    gr[z, rows(0, yl, 128), :] = grad_out[:, lanes(yl)]

    attend_both(2)
    a3 = ring_step(kv, 3, a2)
    b2 = ring_step(qs, 2, b1)
    g_swap.wait_recv()
    g0 = ring_step(gr, 0, [])
    attend_both(3)
    wait_all(a3)
    attend(at_z(4))

    heads = [acc_s[i] / l_s[i] for i in range(2)]
    logs = [m_s[i] + jnp.log(l_s[i]) for i in range(2)]
    att = (heads[0] + heads[1]).astype(BF16)
    att_out[...] = att
    t_swap = send(att_out, att_own.at[1], mate_y)
    g_own = gr[z].astype(F32)
    dots = [jnp.sum(g_own * heads[i], axis=1, keepdims=True) for i in range(2)]
    lane = lax.broadcasted_iota(jnp.int32, (256, HD), 1)
    table = jnp.zeros((256, HD), F32)
    for i, column in enumerate(logs + dots):
        table = jnp.where(lane == i, column, table)
    st[z] = table.T[0:8, :]
    s_copies = [send(st.at[z], st.at[z], {"z": at_z(d)}) for d in range(1, NZ)]
    b3 = ring_step(qs, 3, b2)
    g1 = ring_step(gr, 1, g0)

    t_swap.wait_recv()
    for half in range(2):
        a_rows = pl.ds(half * 128, 128)
        att_all[half, z, :, lanes(yl)] = att_out[a_rows, :]
        att_all[half, z, :, lanes(1 - yl)] = att_own[1, a_rows, :]

    def att_step(s, before):
        wait_all(before)
        right, left = {"z": at_z(1)}, {"z": at_z(-1)}
        from_r, from_l = at_z(-s), at_z(s)
        last = s == NZ // 2 - 1
        made = []
        for half in range(2):
            if not (last and half == 1):
                made.append(send(att_all.at[half, from_r], att_all.at[half, from_r], right))
            if not (last and half == 0):
                made.append(send(att_all.at[half, from_l], att_all.at[half, from_l], left))
        return made

    t0 = att_step(0, [])

    own_att = att_all[yl, z]
    for b in range(8):
        part[b] = dot(own_att, w[:, 640 * b : 640 * (b + 1)]).astype(BF16)
    p_core = [
        send(part.at[2 * i + (1 - core)], core_in.at[i], mate_c) for i in range(NX)
    ]

    def query_side(o, carry):
        g = gr[z]
        p = jnp.exp(self_s[o] - logs[0])
        d = dot_t(g, kv[o, V0 : V0 + 256, :])
        ds = (p * (d - dots[0])).astype(BF16)
        dqa[0] += dot(ds, kv[o, K0 : K0 + 256, :])
        p = jnp.exp(cross_s[o] - logs[1])
        d = dot_t(g, kv[o, HV0 : HV0 + 384, :])
        ds = (p * (d - dots[1])).astype(BF16)
        dqa[1] += dot(ds, kv[o, HK0 : HK0 + 384, :])
        return carry

    dqa[...] = jnp.zeros(dqa.shape, F32)
    lax.fori_loop(0, 4, query_side, 0)

    wait_all(p_core)

    def add_cores(i, carry):
        both = part[2 * i + core].astype(F32) + core_in[i].astype(F32)
        mid[i] = both.astype(BF16)
        return carry

    lax.fori_loop(0, NX, add_cores, 0)
    p_x = [send(mid.at[at_x(d)], x_in.at[d - 1], {"x": at_x(d)}) for d in (1, 3, 2)]
    g2 = ring_step(gr, 2, g1)
    t1 = att_step(1, t0)

    lax.fori_loop(4, 8, query_side, 0)
    g3 = ring_step(gr, 3, g2)
    t2 = att_step(2, t1)

    def give_back(i, values):
        base, n = OUT_AT[i]
        xo[base : base + 2 * n, :] = values.astype(BF16)
        at = rows(base, 1 - yl, n)
        return send(xo.at[at], xi.at[at], mate_y)

    backs = [(oq, 0, give_back(0, dqa[0] * FACTOR)), (ocq, 1, give_back(1, dqa[1] * FACTOR))]

    wait_all(s_copies)
    ka[...] = jnp.zeros(ka.shape, F32)

    def key_side(o):
        g = gr[o]
        keep = (col[:, 1:2] <= row[o, 0:1, :]) | (col[:, 2:3] == row[o, 2:3, :])
        s = jnp.where(keep, dot_t(kv[z, K0 : K0 + 256, :], qs[o, 0:256, :]) * FACTOR, HIDDEN)
        for qq, stat, at_k, at_v, n in ((qs[o, 0:256, :], 0, K0, V0, 256), (qs[o, 256:512, :], 1, HK0, HV0, 384)):
            if stat == 1:
                s = dot_t(kv[z, at_k : at_k + n, :], qq) * FACTOR
            p = jnp.exp(s - st[o, stat : stat + 1, :])
            ka[at_v : at_v + n, :] += dot(p.astype(BF16), g)
            d = dot_t(kv[z, at_v : at_v + n, :], g)
            ds = (p * (d - st[o, stat + 2 : stat + 3, :])).astype(BF16)
            ka[at_k : at_k + n, :] += dot(ds, qq)

    def keys_both(first, count):
        def body(i, carry):
            d = first + lax.div(i, 2)
            sign = 1 - 2 * lax.rem(i, 2)
            key_side(lax.rem(z + NZ + d * sign, NZ))
            return carry

        lax.fori_loop(0, 2 * count, body, 0)

    key_side(z)
    keys_both(1, 2)

    wait_all(p_x)
    total = mid[x].astype(F32)
    for d in range(3):
        total = total + x_in[d].astype(F32)

    @pl.when(yh == 0)
    def _():
        y_out[0] = total[:, 0:320]
        y_out[1] = total[:, 320:640]

    @pl.when(yh == 1)
    def _():
        y_out[0] = total[:, 320:640]
        y_out[1] = total[:, 0:320]

    y_in[0] = y_out[1].astype(BF16)
    p_y = send(y_in.at[0], y_in.at[1], mate_h)

    wait_all(b3)
    t3 = att_step(3, t2)
    keys_both(3, 1)
    wait_all(g3)
    key_side(at_z(4))

    for i, ref, base, n, scale in ((2, ok, K0, 256, FACTOR), (3, ov, V0, 256, 1.0), (4, ohk, HK0, 384, FACTOR), (5, ohv, HV0, 384, 1.0)):
        backs.append((ref, i, give_back(i, ka[base : base + n, :] * scale)))

    p_y.wait_recv()
    out[...] = (y_out[0] + y_in[1].astype(F32)).astype(BF16)
    for ref, i, copy in backs:
        base, n = OUT_AT[i]
        copy.wait_recv()
        ref[:, lanes(yl)] = xo[rows(base, yl, n), :]
        ref[:, lanes(1 - yl)] = xi[rows(base, yl, n), :]
    wait_all(t3)
    for copy in started:
        copy.wait_send()


def on_device(q, k, v, cq, hk, hv, frame_ids, masked, w, cot):
    z = lax.axis_index("z")
    frames = frame_ids.astype(F32)
    key_frames = jnp.where(masked == 0, frames, NEVER)
    place = jnp.arange(frames.shape[0], dtype=jnp.int32).astype(F32)

    def by_z(a):
        return a.reshape(2, NZ, 128).transpose(1, 0, 2).reshape(NZ, 256)

    info = jnp.stack([by_z(frames), by_z(key_frames), by_z(place)], axis=1)
    row = jnp.pad(info, ((0, 0), (0, 5), (0, 0)))
    own = lax.dynamic_index_in_dim(info, z, 0, keepdims=False)
    col = jnp.pad(own.T, ((0, 0), (0, HD - 3)))

    swap = [(i, (i % 16) * 16 + i // 16) for i in range(256)]
    turned = lax.ppermute(cot, AXES, swap)
    tall = lax.all_gather(turned, COLS, axis=0, tiled=True)

    vmem = pl.BlockSpec(memory_space=pltpu.VMEM)
    shape = jax.ShapeDtypeStruct
    results = pl.pallas_call(
        kernel,
        out_shape=(
            shape((128, 320), BF16),
            *[shape((128, 256), BF16)] * 4,
            *[shape((192, 256), BF16)] * 2,
            shape((2, NZ, 128, 256), BF16),
        ),
        in_specs=[vmem] * 6 + [pl.BlockSpec(memory_space=pl.ANY)] + [vmem] * 3,
        out_specs=[vmem] * 8,
        scratch_shapes=[
            pltpu.VMEM((NZ, KV_ROWS, HD), BF16),
            pltpu.VMEM((NZ, 512, HD), BF16),
            pltpu.VMEM((NZ, 256, HD), BF16),
            pltpu.VMEM((NZ, 8, 256), F32),
            pltpu.VMEM((NZ, 256, 256), F32),
            pltpu.VMEM((NZ, 256, 384), F32),
            pltpu.VMEM((2, 256, 1), F32),
            pltpu.VMEM((2, 256, 1), F32),
            pltpu.VMEM((2, 256, HD), F32),
            pltpu.VMEM((256, 5120), BF16),
            pltpu.VMEM((128, 320), BF16),
            pltpu.VMEM((8, 128, 640), BF16),
            pltpu.VMEM((8, 128, 640), BF16),
            pltpu.VMEM((NX, 128, 640), BF16),
            pltpu.VMEM((NX, 128, 640), BF16),
            pltpu.VMEM((NX - 1, 128, 640), BF16),
            pltpu.VMEM((2, 128, 320), F32),
            pltpu.VMEM((2, 128, 320), BF16),
            pltpu.VMEM((128, 256), BF16),
            pltpu.VMEM((2, 256, HD), BF16),
            pltpu.VMEM((256, HD), BF16),
            pltpu.VMEM((KV_ROWS, HD), F32),
            pltpu.VMEM((2, 256, HD), F32),
            pltpu.VMEM((OUT_ROWS, HD), BF16),
            pltpu.VMEM((OUT_ROWS, HD), BF16),
            pltpu.SemaphoreType.DMA((96,)),
            pltpu.SemaphoreType.DMA((96,)),
            pltpu.SemaphoreType.DMA((1,)),
        ],
        compiler_params=pltpu.CompilerParams(
            collective_id=0, has_side_effects=True, vmem_limit_bytes=50 * 2**20
        ),
        cost_estimate=pl.CostEstimate(
            flops=4_000_000_000, bytes_accessed=10_000_000, transcendentals=3_000_000
        ),
    )(q, k, v, cq, hk, hv, w, cot, row, col)
    att = results[7].reshape(2048, 256)
    weight_grad = lax.dot_general(
        att, tall, (((0,), (0,)), ((), ())), preferred_element_type=F32
    )
    return (*results[:7], weight_grad)


def solution(mesh):
    finer = Mesh(mesh.devices.reshape(2, NZ, NX, 2, 2), AXES)
    split = P(GRP, COLS)
    return jax.shard_map(
        on_device,
        mesh=finer,
        in_specs=(*[split] * 6, P(), P(), P(COLS, None), split),
        out_specs=(*[split] * 7, P(COLS, GRP)),
        check_vma=False,
    )
```

time: 274 us -> 126 us (0.46)
  waiting for transfers between devices: 110 us -> 4.9 us
  Pallas kernels: 0 us -> 85 us
  local copies, waits for them, and re-layouts: 55.7 us -> 11.5 us
  blocking collectives: 36.1 us -> 0 us
  matrix products: 33.8 us -> 2.54 us
  starting transfers between devices: 12.8 us -> 4.85 us
  other arithmetic: 8.33 us -> 1.47 us
    pallas_call x0 -> x1, Pallas kernels: none -> 85 us  [on_device(): pl.pallas_call(kernel, out_shape=(shape((128, 320), BF16), *[shape((128,...]
    all_gather x2 -> x1, waiting for transfers between devices: 75.9 us -> 0.01 us  [on_device(): tall = lax.all_gather(turned, COLS, axis=0, tiled=True)]
    all_gather x1 -> x0, blocking collectives: 36.1 us -> none  [side_by_side(): result = lax.all_gather(both, axis, axis=dim, tiled=True)]
    dot_general x17 -> x1, matrix products: 33.8 us -> 2.54 us  [on_device(): lax.dot_general(att, tall, (((0,), (0,)), ((), ())), preferred_element_ty...]
    all_to_all x2 -> x0, waiting for transfers between devices: 26.6 us -> none  [the longest x1 26.6 us: from_everyone(): lax.all_to_all(jnp.broadcast_to(array[None], (length, *array.shape)), axi...]
    another operation x6 -> x0, local copies, waits for them, and re-layouts: 16.5 us -> none  [split_heads(): return matrix.reshape(matrix.shape[0], matrix.shape[1] // HD, HD)]
    all_to_all x2 -> x0, starting transfers between devices: 12.5 us -> none  [the longest x1 6.34 us: summed_on_arrival(): lax.all_to_all(split_up(array, dim, length), axis, 0, 0, tiled=True)]
    reduce_scatter x2 -> x0, waiting for transfers between devices: 7.22 us -> none  [reduced_to_own(): pieces = lax.psum_scatter(pieces, axes[k], scatter_dimension=0, tiled=True)]
  transfers between devices with their start and end apart: 6 -> 2, of which waited for: 4 -> 1; matrix products, arithmetic and copies ran while one was open for 32% -> 3% of each run, Pallas kernels for 0% -> 68%
where the time goes in v1:
time: 126 us; the launch traced here: 124 us
  Pallas kernels  85 us (67%)
  between operations  14.1 us (11%)
  local copies, waits for them, and re-layouts  11.5 us (9%)
  waiting for transfers between devices  4.9 us (4%)
  starting transfers between devices  4.85 us (4%)
  matrix products  2.54 us (2%)
  other arithmetic  1.47 us (1%)
    pallas_call x1, Pallas kernels, on_device(): pl.pallas_call(kernel, out_shape=(shape((128, 320), BF16), *[shape((128,...  85 us
    unnamed x22, local copies, waits for them, and re-layouts  11.3 us
    ppermute x1, waiting for transfers between devices, on_device(): turned = lax.ppermute(cot, AXES, swap)  4.89 us
    ppermute x1, starting transfers between devices, on_device(): turned = lax.ppermute(cot, AXES, swap)  4.82 us
    dot_general x1, matrix products, on_device(): lax.dot_general(att, tall, (((0,), (0,)), ((), ())), preferred_element_ty...  2.54 us
  transfers between devices with their start and end apart: 2, of which 1 were waited for; matrix products, arithmetic and copies ran while one was open for 3% of the time, Pallas kernels for 68%

profile of v1, /device:TPU:8, one launch (start us, length us, event | category | flops | bytes accessed | tf_op | source)
XLA Modules:
  0.0 124.3 jit_solution(3979743156536801791)
XLA Ops:
  7.2 0.0 all-gather.2.cloned.1.call-start
  7.2 4.8 %collective-permute-start = (bf16[128,320]{0,1:T(8,128)(2,1)}, bf16[128,320]{0,1:T(8,128)(2,1)S(1)}, u32[]{:S(2)}, u32[]{:S(2)}) collective-permute-start(bf16[128,320]{0,1:T(8,128)(2,1)} %param.19), channel_id=1, source_target_pairs={{0,0},{1,16},{2,32},{3,48},{4,64},{5,80},{6,96},{7,112},{8,128},{9... | collective-permute-start | bytes 245768 | tf_op jit(solution)/shard_map/ppermute | solution.py:360
  12.0 4.9 %collective-permute-done = bf16[128,320]{0,1:T(8,128)(2,1)S(1)} collective-permute-done((bf16[128,320]{0,1:T(8,128)(2,1)}, bf16[128,320]{0,1:T(8,128)(2,1)S(1)}, u32[]{:S(2)}, u32[]{:S(2)}) %collective-permute-start) | collective-permute-done | bytes 81952 | tf_op jit(solution)/shard_map/ppermute | solution.py:360
  16.9 0.0 copy-start.6
  16.9 0.6 copy-done.6
  17.6 0.0 all-gather.2.cloned.1.call-update
  17.6 1.0 copy.30.cot
  18.6 0.7 select_bitcast_fusion
  19.3 0.7 convert_bitcast_fusion
  20.1 0.1 copy.29
  20.3 0.0 copy-start
  20.3 0.9 copy-done
  21.2 0.0 copy-start.1
  21.2 0.9 copy-done.1
  22.1 0.0 copy-start.2
  22.1 0.8 copy-done.2
  22.9 0.0 copy-start.3
  22.9 0.8 copy-done.3
  23.8 0.0 copy-start.4
  23.8 0.8 copy-done.4
  24.6 0.0 copy-start.5
  24.6 0.8 copy-done.5
  25.4 85.0 %shard_map.161 = (bf16[128,320]{1,0:T(8,128)(2,1)S(1)}, bf16[128,256]{1,0:T(8,128)(2,1)S(1)}, bf16[128,256]{1,0:T(8,128)(2,1)S(1)}, bf16[128,256]{1,0:T(8,128)(2...) custom-call(bf16[128,256]{1,0:T(8,128)(2,1)S(1)} %copy-done.2, ...), custom_call_target="tpu_custom_call" | custom-call | flops 4000000000 | bytes 10000000 | tf_op jit(solution)/shard_map/pallas_call | solution.py:365
  110.4 0.7 copy.31
  111.2 0.0 all-gather.2.cloned.1.call-done
  111.2 2.5 %fusion = f32[256,320]{0,1:T(8,128)} fusion(bf16[2048,320]{0,1:T(8,128)(2,1)} %all-gather.2.cloned.1.call-done, bf16[2048,256]{1,0:T(8,128)(2,1)S(1)} %bitcast.20), kind=kOutput, calls=%fused_computation.7 | convolution fusion | flops 335544320 | bytes 2686976 | tf_op jit(solution)/shard_map/dot_general | solution.py:413
  113.7 0.6 copy.38
  114.3 0.6 copy.39
  115.0 0.6 copy.40
  115.6 0.6 copy.41
  116.2 0.6 copy.42
  116.9 0.6 copy.43
  (8 shorter events, 0.1 us)
Async XLA Ops:
  7.2 104.0 %all-gather.2.cloned.1.call-start = ((), (), s32[]{:S(2)}) async-start(), calls=%async_computation | async-start | bytes 1392640 | tf_op jit(solution)/shard_map/all_gather | solution.py:361
  7.2 9.7 %collective-permute-start = (bf16[128,320]{0,1:T(8,128)(2,1)}, bf16[128,320]{0,1:T(8,128)(2,1)S(1)}, u32[]{:S(2)}, u32[]{:S(2)}) collective-permute-start(bf16[128,320]{0,1:T(8,128)(2,1)} %param.19), channel_id=1, source_target_pairs={{0,0},{1,16},{2,32},{3,48},{4,64},{5,80},{6,96},{7,112},{8,128},{9... | collective-permute-start | bytes 245768 | tf_op jit(solution)/shard_map/ppermute | solution.py:360
  16.9 0.6 copy-start.6
  20.3 0.9 copy-start
  21.2 0.9 copy-start.1
  22.1 0.8 copy-start.2
  22.9 0.8 copy-start.3
  23.8 0.8 copy-start.4
  24.6 0.8 copy-start.5
Sparse Core Ops, SparseCore 0:
  17.7 58.4 all-gather.1

commit v2 on v1

v2 whole, which is shorter than its diff:
```python
import itertools

import jax
import jax.numpy as jnp
from jax import lax
from jax.experimental import pallas as pl
from jax.experimental.pallas import tpu as pltpu
from jax.sharding import Mesh
from jax.sharding import PartitionSpec as P

F32, BF16 = jnp.float32, jnp.bfloat16
HD = 128
FACTOR = HD**-0.5
NZ, NX = 8, 4
HIDDEN = -1e30
NEVER = 1e9
MESH = pl.DeviceIdType.MESH
AXES = ("yl", "z", "x", "core", "yh")
GRP, COLS = ("yl", "z"), ("x", "core", "yh")

K0, V0, HK0, HV0, KV_ROWS = 0, 256, 512, 896, 1280
OUT_AT = ((0, 128), (256, 128), (512, 128), (768, 128), (1024, 192), (1408, 192))
OUT_ROWS = 1792
TURN, TURN_OWN = 127, 31


def dot(a, b):
    return lax.dot_general(a, b, (((1,), (0,)), ((), ())), preferred_element_type=F32)


def dot_t(a, b):
    return lax.dot_general(a, b, (((1,), (1,)), ((), ())), preferred_element_type=F32)


def kernel(
    q, k, v, cq, hk, hv, w_hbm, cot, frames, masked,
    out_h, oq_h, ok_h, ov_h, ocq_h, ohk_h, ohv_h, wg_h,
    out, oq, ok, ov, ocq, ohk, ohv, wg, att_all, tall, kv, qs, gr, st, self_s, cross_s, m_s, l_s, acc_s, w, cf, part, core_in,
    mid, x_in, y_out, y_in, grad_out, ka, dqa, xo, xi, row_q, row_k, row_p, col,
    send_sems, recv_sems, own_sems,
):
    yl, z, x = lax.axis_index("yl"), lax.axis_index("z"), lax.axis_index("x")
    core, yh = lax.axis_index("core"), lax.axis_index("yh")
    mate_y, mate_c, mate_h = {"yl": 1 - yl}, {"core": 1 - core}, {"yh": 1 - yh}
    blk = x * 2 + core
    tokens, chunk = yl * NZ + z, blk * 2 + yh
    turned = {
        "yl": lax.div(chunk, NZ), "z": lax.rem(chunk, NZ), "x": lax.div(tokens, 4),
        "core": lax.rem(lax.div(tokens, 2), 2), "yh": lax.rem(tokens, 2),
    }

    def at_z(d):
        return lax.rem(z + (d + NZ), NZ)

    def at_x(d):
        return lax.rem(x + (d + NX), NX)

    peers = [mate_y, mate_c, mate_h]
    peers += [{"z": at_z(d)} for d in range(1, NZ)] + [{"x": at_x(d)} for d in range(1, NX)]
    barrier = pltpu.get_barrier_semaphore()
    for peer in peers:
        pl.semaphore_signal(barrier, inc=1, device_id=peer, device_id_type=MESH)

    @pl.when(tokens != chunk)
    def _():
        pl.semaphore_signal(barrier, inc=1, device_id=turned, device_id_type=MESH)

    own_number = itertools.count()

    def bring(src, dst):
        copy = pltpu.make_async_copy(src, dst, own_sems.at[next(own_number)])
        copy.start()
        return copy

    def lanes(i):
        return pl.ds(pl.multiple_of(i * HD, HD), HD)

    def rows(base, i, n):
        return pl.ds(pl.multiple_of(base + i * n, 16), n)

    owned = ((k, kv, K0, 128), (hk, kv, HK0, 192), (v, kv, V0, 128), (hv, kv, HV0, 192), (q, qs, 0, 128), (cq, qs, 256, 128))
    brought = [bring(src.at[:, lanes(yl)], dst.at[z, rows(base, yl, n)]) for src, dst, base, n in owned]
    cot_own = bring(cot, cf.at[chunk])
    w_copy = bring(w_hbm, w)
    pl.semaphore_wait(barrier, len(peers) + (tokens != chunk).astype(jnp.int32))

    number = itertools.count()
    started = []

    def send(src, dst, to):
        i = next(number)
        copy = pltpu.make_async_remote_copy(
            src_ref=src, dst_ref=dst, send_sem=send_sems.at[i], recv_sem=recv_sems.at[i],
            device_id=to, device_id_type=MESH,
        )
        copy.start()
        started.append(copy)
        return copy

    cot_copy = send(cot, cf.at[chunk], mate_h)
    swaps = [
        send(src.at[:, lanes(1 - yl)], dst.at[z, rows(base, yl, n)], mate_y)
        for src, dst, base, n in owned
    ]
    t_copy = pltpu.make_async_remote_copy(
        src_ref=cot, dst_ref=tall.at[tokens], send_sem=send_sems.at[TURN], recv_sem=recv_sems.at[TURN],
        device_id=turned, device_id_type=MESH,
    )
    t_own = pltpu.make_async_copy(cot, tall.at[tokens], own_sems.at[TURN_OWN])

    @pl.when(tokens != chunk)
    def _():
        t_copy.start()

    @pl.when(tokens == chunk)
    def _():
        t_own.start()

    lane = lax.broadcasted_iota(jnp.int32, (NZ, 256), 1)
    place = lax.broadcasted_iota(jnp.int32, (NZ, 256), 0) * 128 + lane
    place = jnp.where(lane < 128, place, place + (NZ * 128 - 128))
    row_p[...] = place.astype(F32)
    own_frames = frames[...].astype(F32)
    key_frames = jnp.where(masked[...] == 0, own_frames, NEVER)
    row_q[...] = jnp.concatenate([own_frames[0:NZ], own_frames[NZ : 2 * NZ]], axis=1)
    row_k[...] = jnp.concatenate([key_frames[0:NZ], key_frames[NZ : 2 * NZ]], axis=1)
    which = lax.broadcasted_iota(jnp.int32, (HD, 256), 0)
    spread = jnp.where(which == 0, row_q[pl.ds(z, 1), :], row_k[pl.ds(z, 1), :])
    col[...] = jnp.where(which == 2, row_p[pl.ds(z, 1), :], spread).T

    def ring_step(view, s, before):
        for copy in before:
            copy.wait_recv()
        right, left = {"z": at_z(1)}, {"z": at_z(-1)}
        last = s == NZ // 2 - 1
        from_r, from_l = view(at_z(-s), 0 if last else None), view(at_z(s), 1 if last else None)
        return [send(from_r, from_r, right), send(from_l, from_l, left)]

    def whole_or_half(ref):
        half = ref.shape[1] // 2

        def view(o, part):
            return ref.at[o] if part is None else ref.at[o, pl.ds(part * half, half)]

        return view

    kv_view, qs_view, gr_view = whole_or_half(kv), whole_or_half(qs), whole_or_half(gr)

    def att_view(o, part):
        return att_all.at[slice(None) if part is None else part, o, :, lanes(yl)]

    def wait_all(copies):
        for copy in copies:
            copy.wait_recv()

    m_s[...] = jnp.full(m_s.shape, HIDDEN, F32)
    l_s[...] = jnp.zeros(l_s.shape, F32)
    acc_s[...] = jnp.zeros(acc_s.shape, F32)

    def take_in(i, s, values):
        top = m_s[i]
        new = jnp.maximum(top, jnp.max(s, axis=1, keepdims=True))
        p = jnp.exp(s - new)
        shrink = jnp.exp(top - new)
        l_s[i] = l_s[i] * shrink + jnp.sum(p, axis=1, keepdims=True)
        acc_s[i] = acc_s[i] * shrink + dot(p.astype(BF16), values)
        m_s[i] = new

    def attend(o):
        s = dot_t(qs[z, 0:256, :], kv[o, K0 : K0 + 256, :]) * FACTOR
        keep = (row_k[pl.ds(o, 1), :] <= col[:, 0:1]) | (row_p[pl.ds(o, 1), :] == col[:, 2:3])
        s = jnp.where(keep, s, HIDDEN)
        self_s[o] = s
        take_in(0, s, kv[o, V0 : V0 + 256, :])
        s = dot_t(qs[z, 256:512, :], kv[o, HK0 : HK0 + 384, :]) * FACTOR
        cross_s[o] = s
        take_in(1, s, kv[o, HV0 : HV0 + 384, :])

    def attend_both(d):
        def body(i, carry):
            attend(lax.rem(z + NZ + d * (1 - 2 * i), NZ))
            return carry

        lax.fori_loop(0, 2, body, 0)

    for copy in brought[0:4]:
        copy.wait()
    wait_all(swaps[0:4])
    a0 = ring_step(kv_view, 0, [])
    for copy in brought[4:6]:
        copy.wait()
    wait_all(swaps[4:6])
    b0 = ring_step(qs_view, 0, [])

    def pair(ref, d):
        return ref.at[pl.ds((at_x(d) * 2 + core) * 2, 2)]

    def one(ref, d, i):
        return ref.at[(at_x(d) * 2 + core) * 2 + i]

    def x_first(ref):
        mine = pair(ref, 0)
        return [send(mine, mine, {"x": at_x(1)}), send(mine, mine, {"x": at_x(-1)}), send(mine, mine, mate_c)]

    def x_second(ref, before):
        before[0].wait_recv()
        far = one(ref, -1, 0)
        made = [send(far, far, {"x": at_x(1)})]
        cores = [before[2], send(pair(ref, -1), pair(ref, -1), mate_c)]
        before[1].wait_recv()
        far = one(ref, 1, 1)
        made.append(send(far, far, {"x": at_x(-1)}))
        cores.append(send(pair(ref, 1), pair(ref, 1), mate_c))
        return made, cores

    def x_third(ref, before):
        made, cores = before
        wait_all(made)
        return cores + [send(pair(ref, 2), pair(ref, 2), mate_c)]

    cot_own.wait()
    cot_copy.wait_recv()
    c_first = x_first(cf)
    attend(z)
    c_second = x_second(cf, c_first)
    a1 = ring_step(kv_view, 1, a0)

    @pl.when(tokens != chunk)
    def _():
        t_copy.wait()

    @pl.when(tokens == chunk)
    def _():
        t_own.wait()

    turn_h = send(tall.at[chunk], tall.at[chunk], mate_h)
    attend_both(1)
    c_core = x_third(cf, c_second)
    a2 = ring_step(kv_view, 2, a1)
    b1 = ring_step(qs_view, 1, b0)
    turn_h.wait_recv()
    turn_first = x_first(tall)

    wait_all(c_core)
    w_copy.wait()
    grad = dot(w[:, 0:640], cf[0:2].reshape(640, HD))
    for b in range(1, 8):
        grad = grad + dot(w[:, 640 * b : 640 * (b + 1)], cf[2 * b : 2 * b + 2].reshape(640, HD))
    grad_out[...] = grad.T.astype(BF16)
    g_swap = send(grad_out.at[:, lanes(1 - yl)], gr.at[z, rows(0, yl, 128)], mate_y)
    gr[z, rows(0, yl, 128), :] = grad_out[:, lanes(yl)]

    attend_both(2)
    a3 = ring_step(kv_view, 3, a2)
    b2 = ring_step(qs_view, 2, b1)
    g_swap.wait_recv()
    g0 = ring_step(gr_view, 0, [])
    turn_second = x_second(tall, turn_first)
    attend_both(3)
    wait_all(a3)
    attend(at_z(4))

    heads = [acc_s[i] / l_s[i] for i in range(2)]
    logs = [m_s[i] + jnp.log(l_s[i]) for i in range(2)]
    att = (heads[0] + heads[1]).astype(BF16)
    for half in range(2):
        att_all[half, z, :, lanes(yl)] = att[half * 128 : half * 128 + 128]

    def to_mate(o):
        return send(att_view(o, None), att_view(o, None), mate_y)

    t_mate = [to_mate(z)]
    g_own = gr[z].astype(F32)
    dots = [jnp.sum(g_own * heads[i], axis=1, keepdims=True) for i in range(2)]
    lane = lax.broadcasted_iota(jnp.int32, (256, HD), 1)
    table = jnp.zeros((256, HD), F32)
    for i, column in enumerate(logs + dots):
        table = jnp.where(lane == i, column, table)
    st[z] = table.T[0:8, :]
    s_copies = [send(st.at[z], st.at[z], {"z": at_z(d)}) for d in range(1, NZ)]
    b3 = ring_step(qs_view, 3, b2)
    g1 = ring_step(gr_view, 1, g0)

    t0 = ring_step(att_view, 0, [])
    turn_core = x_third(tall, turn_second)
    t_mate[0].wait_recv()

    own_att = att_all[yl, z]
    for b in range(8):
        part[b] = dot(own_att, w[:, 640 * b : 640 * (b + 1)]).astype(BF16)
    p_core = [
        send(part.at[2 * i + (1 - core)], core_in.at[i], mate_c) for i in range(NX)
    ]

    def query_side(o, carry):
        g = gr[z]
        p = jnp.exp(self_s[o] - logs[0])
        d = dot_t(g, kv[o, V0 : V0 + 256, :])
        ds = (p * (d - dots[0])).astype(BF16)
        dqa[0] += dot(ds, kv[o, K0 : K0 + 256, :])
        p = jnp.exp(cross_s[o] - logs[1])
        d = dot_t(g, kv[o, HV0 : HV0 + 384, :])
        ds = (p * (d - dots[1])).astype(BF16)
        dqa[1] += dot(ds, kv[o, HK0 : HK0 + 384, :])
        return carry

    dqa[...] = jnp.zeros(dqa.shape, F32)
    lax.fori_loop(0, 4, query_side, 0)

    wait_all(p_core)

    def add_cores(i, carry):
        both = part[2 * i + core].astype(F32) + core_in[i].astype(F32)
        mid[i] = both.astype(BF16)
        return carry

    lax.fori_loop(0, NX, add_cores, 0)
    p_x = [send(mid.at[at_x(d)], x_in.at[d - 1], {"x": at_x(d)}) for d in (1, 3, 2)]
    g2 = ring_step(gr_view, 2, g1)
    t1 = ring_step(att_view, 1, t0)
    t_mate += [to_mate(at_z(1)), to_mate(at_z(-1))]

    lax.fori_loop(4, 8, query_side, 0)
    g3 = ring_step(gr_view, 3, g2)
    t2 = ring_step(att_view, 2, t1)
    t_mate += [to_mate(at_z(2)), to_mate(at_z(-2))]

    def give_back(i, values):
        base, n = OUT_AT[i]
        xo[base : base + 2 * n, :] = values.astype(BF16)
        at = rows(base, 1 - yl, n)
        return send(xo.at[at], xi.at[at], mate_y)

    backs = [(oq, 0, give_back(0, dqa[0] * FACTOR)), (ocq, 1, give_back(1, dqa[1] * FACTOR))]

    wait_all(s_copies)
    ka[...] = jnp.zeros(ka.shape, F32)

    def key_side(o):
        g = gr[o]
        keep = (col[:, 1:2] <= row_q[pl.ds(o, 1), :]) | (col[:, 2:3] == row_p[pl.ds(o, 1), :])
        s = jnp.where(keep, dot_t(kv[z, K0 : K0 + 256, :], qs[o, 0:256, :]) * FACTOR, HIDDEN)
        for qq, stat, at_k, at_v, n in ((qs[o, 0:256, :], 0, K0, V0, 256), (qs[o, 256:512, :], 1, HK0, HV0, 384)):
            if stat == 1:
                s = dot_t(kv[z, at_k : at_k + n, :], qq) * FACTOR
            p = jnp.exp(s - st[o, stat : stat + 1, :])
            ka[at_v : at_v + n, :] += dot(p.astype(BF16), g)
            d = dot_t(kv[z, at_v : at_v + n, :], g)
            ds = (p * (d - st[o, stat + 2 : stat + 3, :])).astype(BF16)
            ka[at_k : at_k + n, :] += dot(ds, qq)

    def keys_both(first, count):
        def body(i, carry):
            d = first + lax.div(i, 2)
            sign = 1 - 2 * lax.rem(i, 2)
            key_side(lax.rem(z + NZ + d * sign, NZ))
            return carry

        lax.fori_loop(0, 2 * count, body, 0)

    key_side(z)
    keys_both(1, 2)

    wait_all(p_x)
    total = mid[x].astype(F32)
    for d in range(3):
        total = total + x_in[d].astype(F32)
    y_out[...] = total.T
    y_in[0] = y_out[pl.ds(pl.multiple_of((1 - yh) * 320, 64), 320), :].astype(BF16)
    p_y = send(y_in.at[0], y_in.at[1], mate_h)

    wait_all(b3)
    t3 = ring_step(att_view, 3, t2)
    t_mate += [to_mate(at_z(3)), to_mate(at_z(-3))]
    keys_both(3, 1)
    wait_all(t3)
    t_mate.append(to_mate(at_z(4)))
    wait_all(g3)
    key_side(at_z(4))

    for i, ref, base, n, scale in ((2, ok, K0, 256, FACTOR), (3, ov, V0, 256, 1.0), (4, ohk, HK0, 384, FACTOR), (5, ohv, HV0, 384, 1.0)):
        backs.append((ref, i, give_back(i, ka[base : base + n, :] * scale)))

    p_y.wait_recv()
    own_total = y_out[pl.ds(pl.multiple_of(yh * 320, 64), 320), :]
    out[...] = (own_total + y_in[1].astype(F32)).astype(BF16)
    leaving = [bring(out, out_h)]
    for (ref, i, copy), away in zip(backs, (oq_h, ocq_h, ok_h, ov_h, ohk_h, ohv_h)):
        base, n = OUT_AT[i]
        copy.wait_recv()
        ref[:, lanes(yl)] = xo[rows(base, yl, n), :]
        ref[:, lanes(1 - yl)] = xi[rows(base, yl, n), :]
        leaving.append(bring(ref, away))
    wait_all(turn_core)
    wait_all(t_mate[1:])
    total = jnp.zeros((320, 256), F32)
    for half in range(2):
        for o in range(NZ):
            total = total + dot(tall[half * NZ + o], att_all[half, o])
    wg[...] = total
    leaving.append(bring(wg, wg_h))
    for copy in started:
        copy.wait_send()
    for copy in leaving:
        copy.wait()


def finish(*refs):
    sources, outs, held, sems = refs[0:8], refs[8:16], refs[16:24], refs[24]
    inward = [pltpu.make_async_copy(s, h, sems.at[i]) for i, (s, h) in enumerate(zip(sources, held))]
    outward = [pltpu.make_async_copy(h, o, sems.at[8 + i]) for i, (h, o) in enumerate(zip(held, outs))]
    for copy in inward:
        copy.start()
    for copy, onward in zip(inward, outward):
        copy.wait()
        onward.start()
    for copy in outward:
        copy.wait()


def on_device(q, k, v, cq, hk, hv, frame_ids, masked, w, cot):
    vmem = pl.BlockSpec(memory_space=pltpu.VMEM)
    shape = jax.ShapeDtypeStruct
    away = pl.BlockSpec(memory_space=pl.ANY)
    kinds = (shape((320, 128), BF16), *[shape((128, 256), BF16)] * 4, *[shape((192, 256), BF16)] * 2, shape((320, 256), F32))
    results = pl.pallas_call(
        kernel,
        out_shape=kinds,
        in_specs=[away] * 8 + [vmem] * 2,
        out_specs=[away] * 8,
        scratch_shapes=[
            *[pltpu.VMEM(kind.shape, kind.dtype) for kind in kinds],
            pltpu.VMEM((2, NZ, 128, 256), BF16),
            pltpu.VMEM((2 * NZ, 320, HD), BF16),
            pltpu.VMEM((NZ, KV_ROWS, HD), BF16),
            pltpu.VMEM((NZ, 512, HD), BF16),
            pltpu.VMEM((NZ, 256, HD), BF16),
            pltpu.VMEM((NZ, 8, 256), F32),
            pltpu.VMEM((NZ, 256, 256), F32),
            pltpu.VMEM((NZ, 256, 384), F32),
            pltpu.VMEM((2, 256, 1), F32),
            pltpu.VMEM((2, 256, 1), F32),
            pltpu.VMEM((2, 256, HD), F32),
            pltpu.VMEM((256, 5120), BF16),
            pltpu.VMEM((16, 320, HD), BF16),
            pltpu.VMEM((8, 128, 640), BF16),
            pltpu.VMEM((NX, 128, 640), BF16),
            pltpu.VMEM((NX, 128, 640), BF16),
            pltpu.VMEM((NX - 1, 128, 640), BF16),
            pltpu.VMEM((640, HD), F32),
            pltpu.VMEM((2, 320, HD), BF16),
            pltpu.VMEM((128, 256), BF16),
            pltpu.VMEM((KV_ROWS, HD), F32),
            pltpu.VMEM((2, 256, HD), F32),
            pltpu.VMEM((OUT_ROWS, HD), BF16),
            pltpu.VMEM((OUT_ROWS, HD), BF16),
            *[pltpu.VMEM((NZ, 256), F32)] * 3,
            pltpu.VMEM((256, HD), F32),
            pltpu.SemaphoreType.DMA((TURN + 1,)),
            pltpu.SemaphoreType.DMA((TURN + 1,)),
            pltpu.SemaphoreType.DMA((TURN_OWN + 1,)),
        ],
        compiler_params=pltpu.CompilerParams(
            collective_id=0, has_side_effects=True, vmem_limit_bytes=60 * 2**20
        ),
        cost_estimate=pl.CostEstimate(
            flops=4_000_000_000, bytes_accessed=10_000_000, transcendentals=3_000_000
        ),
    )(q, k, v, cq, hk, hv, w, cot.T, frame_ids.reshape(16, 128), masked.reshape(16, 128))
    final = pl.pallas_call(
        finish,
        out_shape=kinds,
        in_specs=[away] * 8,
        out_specs=[away] * 8,
        scratch_shapes=[
            *[pltpu.VMEM(kind.shape, kind.dtype) for kind in kinds],
            pltpu.SemaphoreType.DMA((16,)),
        ],
        compiler_params=pltpu.CompilerParams(vmem_limit_bytes=60 * 2**20),
    )(*results)
    return (final[0].T, *final[1:7], final[7].T)


def solution(mesh):
    finer = Mesh(mesh.devices.reshape(2, NZ, NX, 2, 2), AXES)
    split = P(GRP, COLS)
    return jax.shard_map(
        on_device,
        mesh=finer,
        in_specs=(*[split] * 6, P(), P(), P(COLS, None), split),
        out_specs=(*[split] * 7, P(COLS, GRP)),
        check_vma=False,
    )
```

time: 126 us -> 90.6 us (0.72); the launches traced: 124 us -> 90.3 us
  between operations: 14.1 us -> 0.64 us
  local copies, waits for them, and re-layouts: 11.5 us -> 0 us
  waiting for transfers between devices: 4.9 us -> 0 us
  starting transfers between devices: 4.85 us -> 0 us
  Pallas kernels: 85 us -> 89.7 us
  matrix products: 2.54 us -> 0 us
  other arithmetic: 1.47 us -> 0 us
    unnamed x22 -> x0, local copies, waits for them, and re-layouts: 11.3 us -> none
    ppermute x1 -> x0, waiting for transfers between devices: 4.89 us -> none  [on_device(): turned = lax.ppermute(cot, AXES, swap)]
    ppermute x1 -> x0, starting transfers between devices: 4.82 us -> none  [on_device(): turned = lax.ppermute(cot, AXES, swap)]
    pallas_call x1 -> x2, Pallas kernels: 85 us -> 89.7 us  [the longest x1 87.5 us: on_device(): pl.pallas_call(kernel, out_shape=kinds, in_specs=[away] * 8 + [vmem] * 2,...]
    dot_general x1 -> x0, matrix products: 2.54 us -> none  [on_device(): lax.dot_general(att, tall, (((0,), (0,)), ((), ())), preferred_element_ty...]
    transpose x2 -> x0, other arithmetic: 1.42 us -> none  [by_z(): return a.reshape(2, NZ, 128).transpose(1, 0, 2).reshape(NZ, 256)]
  transfers between devices with their start and end apart: 2 -> 0, of which waited for: 1 -> 0; matrix products, arithmetic and copies ran while one was open for 3% -> 0% of each run, Pallas kernels for 68% -> 0%
where the time goes in v2:
time: 90.6 us; the launch traced here: 90.3 us
  Pallas kernels  89.7 us (99%)
    pallas_call x1, Pallas kernels, on_device(): pl.pallas_call(kernel, out_shape=kinds, in_specs=[away] * 8 + [vmem] * 2,...  87.5 us
    pallas_call x1, Pallas kernels, on_device(): pl.pallas_call(finish, out_shape=kinds, in_specs=[away] * 8, out_specs=[a...  2.12 us

profile of v2, /device:TPU:8, one launch (start us, length us, event | category | flops | bytes accessed | tf_op | source)
XLA Modules:
  0.0 90.3 jit_solution(281079471625860763)
XLA Ops:
  0.6 87.5 %shard_map.161 = (bf16[320,128]{1,0:T(8,128)(2,1)}, bf16[128,256]{1,0:T(8,128)(2,1)}, bf16[128,256]{1,0:T(8,128)(2,1)}, bf16[128,256]{1,0:T(8,128)(2,1)}, bf16[1...) custom-call(bf16[128,256]{1,0:T(8,128)(2,1)} %q.1, ...), custom_call_target="tpu_custom_call" | custom-call | flops 4000000000 | bytes 10000000 | tf_op jit(solution)/shard_map/pallas_call | solution.py:426
  88.2 2.1 %shard_map.162 = (bf16[320,128]{1,0:T(8,128)(2,1)}, bf16[128,256]{1,0:T(8,128)(2,1)}, bf16[128,256]{1,0:T(8,128)(2,1)}, bf16[128,256]{1,0:T(8,128)(2,1)}, bf16[1...) custom-call(bf16[320,128]{1,0:T(8,128)(2,1)} %get-tuple-element.24.refs_0_, ...), custom_call_target="tpu_custom_call" | custom-call | tf_op jit(solution)/shard_map/pallas_call | solution.py:470

commit v3 on v2

--- a/solution.py
+++ b/solution.py
@@ -18,10 +18,10 @@
 AXES = ("yl", "z", "x", "core", "yh")
 GRP, COLS = ("yl", "z"), ("x", "core", "yh")
 
-K0, V0, HK0, HV0, KV_ROWS = 0, 256, 512, 896, 1280
+K0, HK0, V0, HV0, KV_ROWS = 0, 256, 640, 896, 1280
 OUT_AT = ((0, 128), (256, 128), (512, 128), (768, 128), (1024, 192), (1408, 192))
 OUT_ROWS = 1792
-TURN, TURN_OWN = 127, 31
+TURN, TURN_OWN = 127, 47
 
 
 def dot(a, b):
@@ -36,14 +36,27 @@
     q, k, v, cq, hk, hv, w_hbm, cot, frames, masked,
     out_h, oq_h, ok_h, ov_h, ocq_h, ohk_h, ohv_h, wg_h,
     out, oq, ok, ov, ocq, ohk, ohv, wg, att_all, tall, kv, qs, gr, st, self_s, cross_s, m_s, l_s, acc_s, w, cf, part, core_in,
-    mid, x_in, y_out, y_in, grad_out, ka, dqa, xo, xi, row_q, row_k, row_p, col,
+    mid, x_in, y_out, y_in, grad_out, att_out, ka, dqa, xo, row_q, row_k, row_p, col,
     send_sems, recv_sems, own_sems,
 ):
     yl, z, x = lax.axis_index("yl"), lax.axis_index("z"), lax.axis_index("x")
     core, yh = lax.axis_index("core"), lax.axis_index("yh")
+    zp, zq = lax.rem(z, 2), lax.div(z, 2)
+    upper, side = lax.div(z, 4), lax.rem(zq, 2)
     mate_y, mate_c, mate_h = {"yl": 1 - yl}, {"core": 1 - core}, {"yh": 1 - yh}
+    mate_z, next_z = {"z": z + 1 - 2 * zp}, {"z": lax.rem(z + (NZ - 1) + 2 * zp, NZ)}
     blk = x * 2 + core
     tokens, chunk = yl * NZ + z, blk * 2 + yh
+
+    def flip(fz, fy, fc):
+        at = (1 - zp if fz else zp) * 4 + (1 - yl if fy else yl) * 2
+        return at + (1 - core if fc else core)
+
+    slot = flip(0, 0, 0)
+    landing = zp * 4 + yl * 2 + upper
+    swap_to = [{"z": zp + 4 * core + 2 * e, "core": upper} for e in range(2)]
+    stays = [zq == 2 * core + e for e in range(2)]
+
     turned = {
         "yl": lax.div(chunk, NZ), "z": lax.rem(chunk, NZ), "x": lax.div(tokens, 4),
         "core": lax.rem(lax.div(tokens, 2), 2), "yh": lax.rem(tokens, 2),
@@ -55,15 +68,26 @@
     def at_x(d):
         return lax.rem(x + (d + NX), NX)
 
-    peers = [mate_y, mate_c, mate_h]
-    peers += [{"z": at_z(d)} for d in range(1, NZ)] + [{"x": at_x(d)} for d in range(1, NX)]
+    flips = [(fz, fy, fc) for fz in (0, 1) for fy in (0, 1) for fc in (0, 1)][1:]
+    group = [
+        {"z": z + fz * (1 - 2 * zp), "yl": yl + fy * (1 - 2 * yl), "core": core + fc * (1 - 2 * core)}
+        for fz, fy, fc in flips
+    ]
+    peers = [next_z, mate_h] + group + [{"x": at_x(d)} for d in range(1, NX)]
     barrier = pltpu.get_barrier_semaphore()
     for peer in peers:
         pl.semaphore_signal(barrier, inc=1, device_id=peer, device_id_type=MESH)
-
-    @pl.when(tokens != chunk)
-    def _():
-        pl.semaphore_signal(barrier, inc=1, device_id=turned, device_id_type=MESH)
+    expected = len(peers)
+    for peer, here in zip(swap_to + [turned], stays + [tokens == chunk]):
+
+        @pl.when(jnp.logical_not(here))
+        def _():
+            pl.semaphore_signal(barrier, inc=1, device_id=peer, device_id_type=MESH)
+
+        expected = expected + 1 - here.astype(jnp.int32)
+
+    def owner_z(i):
+        return zp + 4 * core + 2 * i
 
     own_number = itertools.count()
 
@@ -78,14 +102,12 @@
     def rows(base, i, n):
         return pl.ds(pl.multiple_of(base + i * n, 16), n)
 
-    owned = ((k, kv, K0, 128), (hk, kv, HK0, 192), (v, kv, V0, 128), (hv, kv, HV0, 192), (q, qs, 0, 128), (cq, qs, 256, 128))
-    brought = [bring(src.at[:, lanes(yl)], dst.at[z, rows(base, yl, n)]) for src, dst, base, n in owned]
     cot_own = bring(cot, cf.at[chunk])
     w_copy = bring(w_hbm, w)
-    pl.semaphore_wait(barrier, len(peers) + (tokens != chunk).astype(jnp.int32))
+    pl.semaphore_wait(barrier, expected)
 
     number = itertools.count()
-    started = []
+    started, exchanged = [], []
 
     def send(src, dst, to):
         i = next(number)
@@ -97,11 +119,62 @@
         started.append(copy)
         return copy
 
+    def exchange(arrays):
+        messages = []
+        for source, target in arrays:
+            first, _ = next(number), next(number)
+            for e in range(2):
+
+                def remote(at, to_slot, to_side, to_owner, e=e, first=first, source=source, target=target):
+                    return pltpu.make_async_remote_copy(
+                        src_ref=source(e), dst_ref=target(to_slot, to_side, to_owner), send_sem=send_sems.at[first + e],
+                        recv_sem=recv_sems.at[first + at], device_id=swap_to[e], device_id_type=MESH,
+                    )
+
+                local = pltpu.make_async_copy(source(e), target(slot, e, z), own_sems.at[next(own_number)])
+                messages.append((e, remote(side, landing, side, owner_z(e)), remote(e, slot, e, z), local))
+        for e in range(2):
+
+            @pl.when(jnp.logical_not(stays[e]))
+            def _():
+                for to, out_copy, _, _ in messages:
+                    if to == e:
+                        out_copy.start()
+
+            @pl.when(stays[e])
+            def _():
+                for to, _, _, local in messages:
+                    if to == e:
+                        local.start()
+
+        exchanged.append(messages)
+        return messages
+
+    def wait_exchange(messages):
+        for e in range(2):
+
+            @pl.when(jnp.logical_not(stays[e]))
+            def _():
+                for to, _, in_copy, _ in messages:
+                    if to == e:
+                        in_copy.wait_recv()
+
+            @pl.when(stays[e])
+            def _():
+                for to, _, _, local in messages:
+                    if to == e:
+                        local.wait()
+
+    def to_slot(src, dst, base, n):
+        return (
+            lambda e: src.at[:, pl.ds(e * HD, HD)],
+            lambda at, i, owner: dst.at[at, rows(base, i, n)],
+        )
+
+    k_moves = exchange([to_slot(k, kv, K0, 128), to_slot(hk, kv, HK0, 192)])
+    v_moves = exchange([to_slot(v, kv, V0, 128), to_slot(hv, kv, HV0, 192)])
     cot_copy = send(cot, cf.at[chunk], mate_h)
-    swaps = [
-        send(src.at[:, lanes(1 - yl)], dst.at[z, rows(base, yl, n)], mate_y)
-        for src, dst, base, n in owned
-    ]
+    q_moves = exchange([to_slot(q, qs, 0, 128), to_slot(cq, qs, 256, 128)])
     t_copy = pltpu.make_async_remote_copy(
         src_ref=cot, dst_ref=tall.at[tokens], send_sem=send_sems.at[TURN], recv_sem=recv_sems.at[TURN],
         device_id=turned, device_id_type=MESH,
@@ -116,17 +189,42 @@
     def _():
         t_own.start()
 
-    lane = lax.broadcasted_iota(jnp.int32, (NZ, 256), 1)
-    place = lax.broadcasted_iota(jnp.int32, (NZ, 256), 0) * 128 + lane
-    place = jnp.where(lane < 128, place, place + (NZ * 128 - 128))
-    row_p[...] = place.astype(F32)
     own_frames = frames[...].astype(F32)
     key_frames = jnp.where(masked[...] == 0, own_frames, NEVER)
-    row_q[...] = jnp.concatenate([own_frames[0:NZ], own_frames[NZ : 2 * NZ]], axis=1)
-    row_k[...] = jnp.concatenate([key_frames[0:NZ], key_frames[NZ : 2 * NZ]], axis=1)
+    lane = lax.broadcasted_iota(jnp.int32, (1, 128), 1)
+    for o in range(8):
+        for i in range(2):
+            t = (o // 2 % 2) * NZ + o // 4 + 4 * (o % 2) + 2 * i
+            at = pl.ds(128 * i, 128)
+            row_q[o : o + 1, at] = own_frames[t : t + 1]
+            row_k[o : o + 1, at] = key_frames[t : t + 1]
+            row_p[o : o + 1, at] = (lane + t * 128).astype(F32)
     which = lax.broadcasted_iota(jnp.int32, (HD, 256), 0)
-    spread = jnp.where(which == 0, row_q[pl.ds(z, 1), :], row_k[pl.ds(z, 1), :])
-    col[...] = jnp.where(which == 2, row_p[pl.ds(z, 1), :], spread).T
+    spread = jnp.where(which == 0, row_q[pl.ds(slot, 1), :], row_k[pl.ds(slot, 1), :])
+    col[...] = jnp.where(which == 2, row_p[pl.ds(slot, 1), :], spread).T
+
+    def part_of(ref, start, n):
+        return lambda o: ref.at[o, pl.ds(start, n)]
+
+    def spread_first(view):
+        mine = view(slot)
+        return [send(mine, mine, mate_z), send(mine, mine, mate_y), send(mine, mine, mate_c)]
+
+    def spread_second(view, before):
+        before[0].wait_recv()
+        got = view(flip(1, 0, 0))
+        made = [send(got, got, mate_y), send(got, got, mate_c)]
+        before[1].wait_recv()
+        got = view(flip(0, 1, 0))
+        return [*made, send(got, got, mate_c)]
+
+    def spread_third(view, before):
+        before[0].wait_recv()
+        got = view(flip(1, 1, 0))
+        return send(got, got, mate_c)
+
+    k_view, v_view = part_of(kv, 0, V0), part_of(kv, V0, V0)
+    q_view, g_view = part_of(qs, 0, 512), part_of(gr, 0, 256)
 
     def ring_step(view, s, before):
         for copy in before:
@@ -136,18 +234,8 @@
         from_r, from_l = view(at_z(-s), 0 if last else None), view(at_z(s), 1 if last else None)
         return [send(from_r, from_r, right), send(from_l, from_l, left)]
 
-    def whole_or_half(ref):
-        half = ref.shape[1] // 2
-
-        def view(o, part):
-            return ref.at[o] if part is None else ref.at[o, pl.ds(part * half, half)]
-
-        return view
-
-    kv_view, qs_view, gr_view = whole_or_half(kv), whole_or_half(qs), whole_or_half(gr)
-
     def att_view(o, part):
-        return att_all.at[slice(None) if part is None else part, o, :, lanes(yl)]
+        return att_all.at[yl, o] if part is None else att_all.at[yl, o, pl.ds(part * 64, 64)]
 
     def wait_all(copies):
         for copy in copies:
@@ -167,30 +255,21 @@
         m_s[i] = new
 
     def attend(o):
-        s = dot_t(qs[z, 0:256, :], kv[o, K0 : K0 + 256, :]) * FACTOR
+        s = dot_t(qs[slot, 0:256, :], kv[o, K0 : K0 + 256, :]) * FACTOR
         keep = (row_k[pl.ds(o, 1), :] <= col[:, 0:1]) | (row_p[pl.ds(o, 1), :] == col[:, 2:3])
         s = jnp.where(keep, s, HIDDEN)
         self_s[o] = s
         take_in(0, s, kv[o, V0 : V0 + 256, :])
-        s = dot_t(qs[z, 256:512, :], kv[o, HK0 : HK0 + 384, :]) * FACTOR
+        s = dot_t(qs[slot, 256:512, :], kv[o, HK0 : HK0 + 384, :]) * FACTOR
         cross_s[o] = s
         take_in(1, s, kv[o, HV0 : HV0 + 384, :])
 
-    def attend_both(d):
+    def both_cores(work, fz, fy):
         def body(i, carry):
-            attend(lax.rem(z + NZ + d * (1 - 2 * i), NZ))
+            work(flip(fz, fy, 0) - core + lax.rem(core + i, 2))
             return carry
 
         lax.fori_loop(0, 2, body, 0)
-
-    for copy in brought[0:4]:
-        copy.wait()
-    wait_all(swaps[0:4])
-    a0 = ring_step(kv_view, 0, [])
-    for copy in brought[4:6]:
-        copy.wait()
-    wait_all(swaps[4:6])
-    b0 = ring_step(qs_view, 0, [])
 
     def pair(ref, d):
         return ref.at[pl.ds((at_x(d) * 2 + core) * 2, 2)]
@@ -218,12 +297,22 @@
         wait_all(made)
         return cores + [send(pair(ref, 2), pair(ref, 2), mate_c)]
 
+    wait_exchange(k_moves)
+    k1 = spread_first(k_view)
+    wait_exchange(v_moves)
+    v1 = spread_first(v_view)
     cot_own.wait()
     cot_copy.wait_recv()
     c_first = x_first(cf)
-    attend(z)
+    wait_exchange(q_moves)
+    q1 = spread_first(q_view)
+    attend(slot)
+    k2 = spread_second(k_view, k1)
     c_second = x_second(cf, c_first)
-    a1 = ring_step(kv_view, 1, a0)
+    v2 = spread_second(v_view, v1)
+    wait_all([k1[2], v1[2]])
+    attend(flip(0, 0, 1))
+    c_core = x_third(cf, c_second)
 
     @pl.when(tokens != chunk)
     def _():
@@ -234,12 +323,6 @@
         t_own.wait()
 
     turn_h = send(tall.at[chunk], tall.at[chunk], mate_h)
-    attend_both(1)
-    c_core = x_third(cf, c_second)
-    a2 = ring_step(kv_view, 2, a1)
-    b1 = ring_step(qs_view, 1, b0)
-    turn_h.wait_recv()
-    turn_first = x_first(tall)
 
     wait_all(c_core)
     w_copy.wait()
@@ -247,43 +330,48 @@
     for b in range(1, 8):
         grad = grad + dot(w[:, 640 * b : 640 * (b + 1)], cf[2 * b : 2 * b + 2].reshape(640, HD))
     grad_out[...] = grad.T.astype(BF16)
-    g_swap = send(grad_out.at[:, lanes(1 - yl)], gr.at[z, rows(0, yl, 128)], mate_y)
-    gr[z, rows(0, yl, 128), :] = grad_out[:, lanes(yl)]
-
-    attend_both(2)
-    a3 = ring_step(kv_view, 3, a2)
-    b2 = ring_step(qs_view, 2, b1)
-    g_swap.wait_recv()
-    g0 = ring_step(gr_view, 0, [])
-    turn_second = x_second(tall, turn_first)
-    attend_both(3)
-    wait_all(a3)
-    attend(at_z(4))
+    g_moves = exchange([to_slot(grad_out, gr, 0, 128)])
+    q2 = spread_second(q_view, q1)
+    wait_all([k2[1], v2[1], k2[2], v2[2]])
+    both_cores(attend, 1, 0)
+    wait_exchange(g_moves)
+    g1 = spread_first(g_view)
+    turn_h.wait_recv()
+    turn_first = x_first(tall)
+    both_cores(attend, 0, 1)
+    k3 = spread_third(k_view, k2)
+    v3 = spread_third(v_view, v2)
+    attend(flip(1, 1, 0))
+    q3 = spread_third(q_view, q2)
+    wait_all([k3, v3])
+    attend(flip(1, 1, 1))
 
     heads = [acc_s[i] / l_s[i] for i in range(2)]
     logs = [m_s[i] + jnp.log(l_s[i]) for i in range(2)]
     att = (heads[0] + heads[1]).astype(BF16)
-    for half in range(2):
-        att_all[half, z, :, lanes(yl)] = att[half * 128 : half * 128 + 128]
+    att_out[...] = att
+    a_moves = exchange(
+        [(lambda e: att_out.at[pl.ds(e * 128, 128)], lambda at, i, owner: att_all.at[yl, owner, :, lanes(i)])]
+    )
 
     def to_mate(o):
         return send(att_view(o, None), att_view(o, None), mate_y)
 
-    t_mate = [to_mate(z)]
-    g_own = gr[z].astype(F32)
+    g_own = gr[slot].astype(F32)
     dots = [jnp.sum(g_own * heads[i], axis=1, keepdims=True) for i in range(2)]
     lane = lax.broadcasted_iota(jnp.int32, (256, HD), 1)
     table = jnp.zeros((256, HD), F32)
     for i, column in enumerate(logs + dots):
         table = jnp.where(lane == i, column, table)
-    st[z] = table.T[0:8, :]
-    s_copies = [send(st.at[z], st.at[z], {"z": at_z(d)}) for d in range(1, NZ)]
-    b3 = ring_step(qs_view, 3, b2)
-    g1 = ring_step(gr_view, 1, g0)
+    st[slot] = table.T[0:8, :]
+    s_copies = [send(st.at[slot], st.at[slot], peer) for peer in group]
+    g2 = spread_second(g_view, g1)
+    turn_second = x_second(tall, turn_first)
+    wait_exchange(a_moves)
 
     t0 = ring_step(att_view, 0, [])
     turn_core = x_third(tall, turn_second)
-    t_mate[0].wait_recv()
+    t_mate = [to_mate(z)]
 
     own_att = att_all[yl, z]
     for b in range(8):
@@ -293,7 +381,7 @@
     ]
 
     def query_side(o, carry):
-        g = gr[z]
+        g = gr[slot]
         p = jnp.exp(self_s[o] - logs[0])
         d = dot_t(g, kv[o, V0 : V0 + 256, :])
         ds = (p * (d - dots[0])).astype(BF16)
@@ -316,22 +404,20 @@
 
     lax.fori_loop(0, NX, add_cores, 0)
     p_x = [send(mid.at[at_x(d)], x_in.at[d - 1], {"x": at_x(d)}) for d in (1, 3, 2)]
-    g2 = ring_step(gr_view, 2, g1)
+    g3 = spread_third(g_view, g2)
     t1 = ring_step(att_view, 1, t0)
     t_mate += [to_mate(at_z(1)), to_mate(at_z(-1))]
 
     lax.fori_loop(4, 8, query_side, 0)
-    g3 = ring_step(gr_view, 3, g2)
     t2 = ring_step(att_view, 2, t1)
     t_mate += [to_mate(at_z(2)), to_mate(at_z(-2))]
 
-    def give_back(i, values):
+    def give_back(i, ref, values):
         base, n = OUT_AT[i]
         xo[base : base + 2 * n, :] = values.astype(BF16)
-        at = rows(base, 1 - yl, n)
-        return send(xo.at[at], xi.at[at], mate_y)
-
-    backs = [(oq, 0, give_back(0, dqa[0] * FACTOR)), (ocq, 1, give_back(1, dqa[1] * FACTOR))]
+        return (lambda e: xo.at[pl.ds(base + e * n, n)], lambda at, j, owner: ref.at[:, lanes(j)])
+
+    dq_moves = exchange([give_back(0, oq, dqa[0] * FACTOR), give_back(1, ocq, dqa[1] * FACTOR)])
 
     wait_all(s_copies)
     ka[...] = jnp.zeros(ka.shape, F32)
@@ -339,27 +425,21 @@
     def key_side(o):
         g = gr[o]
         keep = (col[:, 1:2] <= row_q[pl.ds(o, 1), :]) | (col[:, 2:3] == row_p[pl.ds(o, 1), :])
-        s = jnp.where(keep, dot_t(kv[z, K0 : K0 + 256, :], qs[o, 0:256, :]) * FACTOR, HIDDEN)
+        s = jnp.where(keep, dot_t(kv[slot, K0 : K0 + 256, :], qs[o, 0:256, :]) * FACTOR, HIDDEN)
         for qq, stat, at_k, at_v, n in ((qs[o, 0:256, :], 0, K0, V0, 256), (qs[o, 256:512, :], 1, HK0, HV0, 384)):
             if stat == 1:
-                s = dot_t(kv[z, at_k : at_k + n, :], qq) * FACTOR
+                s = dot_t(kv[slot, at_k : at_k + n, :], qq) * FACTOR
             p = jnp.exp(s - st[o, stat : stat + 1, :])
             ka[at_v : at_v + n, :] += dot(p.astype(BF16), g)
-            d = dot_t(kv[z, at_v : at_v + n, :], g)
+            d = dot_t(kv[slot, at_v : at_v + n, :], g)
             ds = (p * (d - st[o, stat + 2 : stat + 3, :])).astype(BF16)
             ka[at_k : at_k + n, :] += dot(ds, qq)
 
-    def keys_both(first, count):
-        def body(i, carry):
-            d = first + lax.div(i, 2)
-            sign = 1 - 2 * lax.rem(i, 2)
-            key_side(lax.rem(z + NZ + d * sign, NZ))
-            return carry
-
-        lax.fori_loop(0, 2 * count, body, 0)
-
-    key_side(z)
-    keys_both(1, 2)
+    key_side(slot)
+    wait_all([q1[2], g1[2]])
+    key_side(flip(0, 0, 1))
+    wait_all([q2[1], g2[1]])
+    both_cores(key_side, 1, 0)
 
     wait_all(p_x)
     total = mid[x].astype(F32)
@@ -369,38 +449,50 @@
     y_in[0] = y_out[pl.ds(pl.multiple_of((1 - yh) * 320, 64), 320), :].astype(BF16)
     p_y = send(y_in.at[0], y_in.at[1], mate_h)
 
-    wait_all(b3)
     t3 = ring_step(att_view, 3, t2)
     t_mate += [to_mate(at_z(3)), to_mate(at_z(-3))]
-    keys_both(3, 1)
+    wait_all([q2[2], g2[2]])
+    both_cores(key_side, 0, 1)
+    wait_all([q3, g3])
+    both_cores(key_side, 1, 1)
+    dk_moves = exchange(
+        [
+            give_back(2, ok, ka[K0 : K0 + 256, :] * FACTOR),
+            give_back(3, ov, ka[V0 : V0 + 256, :]),
+            give_back(4, ohk, ka[HK0 : HK0 + 384, :] * FACTOR),
+            give_back(5, ohv, ka[HV0 : HV0 + 384, :]),
+        ]
+    )
     wait_all(t3)
     t_mate.append(to_mate(at_z(4)))
-    wait_all(g3)
-    key_side(at_z(4))
-
-    for i, ref, base, n, scale in ((2, ok, K0, 256, FACTOR), (3, ov, V0, 256, 1.0), (4, ohk, HK0, 384, FACTOR), (5, ohv, HV0, 384, 1.0)):
-        backs.append((ref, i, give_back(i, ka[base : base + n, :] * scale)))
 
     p_y.wait_recv()
     own_total = y_out[pl.ds(pl.multiple_of(yh * 320, 64), 320), :]
     out[...] = (own_total + y_in[1].astype(F32)).astype(BF16)
     leaving = [bring(out, out_h)]
-    for (ref, i, copy), away in zip(backs, (oq_h, ocq_h, ok_h, ov_h, ohk_h, ohv_h)):
-        base, n = OUT_AT[i]
-        copy.wait_recv()
-        ref[:, lanes(yl)] = xo[rows(base, yl, n), :]
-        ref[:, lanes(1 - yl)] = xi[rows(base, yl, n), :]
-        leaving.append(bring(ref, away))
+    wait_exchange(dq_moves)
+    leaving += [bring(oq, oq_h), bring(ocq, ocq_h)]
     wait_all(turn_core)
-    wait_all(t_mate[1:])
+    wait_all(t_mate)
     total = jnp.zeros((320, 256), F32)
     for half in range(2):
         for o in range(NZ):
             total = total + dot(tall[half * NZ + o], att_all[half, o])
     wg[...] = total
     leaving.append(bring(wg, wg_h))
+    wait_exchange(dk_moves)
+    leaving += [bring(a, b) for a, b in ((ok, ok_h), (ov, ov_h), (ohk, ohk_h), (ohv, ohv_h))]
     for copy in started:
         copy.wait_send()
+    for e in range(2):
+
+        @pl.when(jnp.logical_not(stays[e]))
+        def _():
+            for messages in exchanged:
+                for to, out_copy, _, _ in messages:
+                    if to == e:
+                        out_copy.wait_send()
+
     for copy in leaving:
         copy.wait()
 
@@ -450,9 +542,9 @@
             pltpu.VMEM((640, HD), F32),
             pltpu.VMEM((2, 320, HD), BF16),
             pltpu.VMEM((128, 256), BF16),
+            pltpu.VMEM((256, HD), BF16),
             pltpu.VMEM((KV_ROWS, HD), F32),
             pltpu.VMEM((2, 256, HD), F32),
-            pltpu.VMEM((OUT_ROWS, HD), BF16),
             pltpu.VMEM((OUT_ROWS, HD), BF16),
             *[pltpu.VMEM((NZ, 256), F32)] * 3,
             pltpu.VMEM((256, HD), F32),

time: 90.6 us -> 83.3 us (0.919)
  Pallas kernels: 89.7 us -> 82.5 us
    pallas_call x1, Pallas kernels: 87.5 us -> 80.4 us  [on_device(): pl.pallas_call(kernel, out_shape=kinds, in_specs=[away] * 8 + [vmem] * 2,...]
where the time goes in v3:
time: 83.3 us; the launch traced here: 83.1 us
  Pallas kernels  82.5 us (99%)
    pallas_call x1, Pallas kernels, on_device(): pl.pallas_call(kernel, out_shape=kinds, in_specs=[away] * 8 + [vmem] * 2,...  80.4 us
    pallas_call x1, Pallas kernels, on_device(): pl.pallas_call(finish, out_shape=kinds, in_specs=[away] * 8, out_specs=[a...  2.12 us

profile of v3, /device:TPU:8, one launch (start us, length us, event | category | flops | bytes accessed | tf_op | source)
XLA Modules:
  0.0 83.1 jit_solution(10654316453622335274)
XLA Ops:
  0.6 80.4 %shard_map.161 = (bf16[320,128]{1,0:T(8,128)(2,1)}, bf16[128,256]{1,0:T(8,128)(2,1)}, bf16[128,256]{1,0:T(8,128)(2,1)}, bf16[128,256]{1,0:T(8,128)(2,1)}, bf16[1...) custom-call(bf16[128,256]{1,0:T(8,128)(2,1)} %q.1, ...), custom_call_target="tpu_custom_call" | custom-call | flops 4000000000 | bytes 10000000 | tf_op jit(solution)/shard_map/pallas_call | solution.py:518
  81.0 2.1 %shard_map.162 = (bf16[320,128]{1,0:T(8,128)(2,1)}, bf16[128,256]{1,0:T(8,128)(2,1)}, bf16[128,256]{1,0:T(8,128)(2,1)}, bf16[128,256]{1,0:T(8,128)(2,1)}, bf16[1...) custom-call(bf16[320,128]{1,0:T(8,128)(2,1)} %get-tuple-element.24.refs_0_, ...), custom_call_target="tpu_custom_call" | custom-call | tf_op jit(solution)/shard_map/pallas_call | solution.py:562

commit v4 on v3

--- a/solution.py
+++ b/solution.py
@@ -171,15 +171,18 @@
             lambda at, i, owner: dst.at[at, rows(base, i, n)],
         )
 
+    def wide(ref, t):
+        return ref.at[lax.div(t, 2), :, lanes(lax.rem(t, 2))]
+
     k_moves = exchange([to_slot(k, kv, K0, 128), to_slot(hk, kv, HK0, 192)])
     v_moves = exchange([to_slot(v, kv, V0, 128), to_slot(hv, kv, HV0, 192)])
     cot_copy = send(cot, cf.at[chunk], mate_h)
     q_moves = exchange([to_slot(q, qs, 0, 128), to_slot(cq, qs, 256, 128)])
     t_copy = pltpu.make_async_remote_copy(
-        src_ref=cot, dst_ref=tall.at[tokens], send_sem=send_sems.at[TURN], recv_sem=recv_sems.at[TURN],
+        src_ref=cot, dst_ref=wide(tall, tokens), send_sem=send_sems.at[TURN], recv_sem=recv_sems.at[TURN],
         device_id=turned, device_id_type=MESH,
     )
-    t_own = pltpu.make_async_copy(cot, tall.at[tokens], own_sems.at[TURN_OWN])
+    t_own = pltpu.make_async_copy(cot, wide(tall, tokens), own_sems.at[TURN_OWN])
 
     @pl.when(tokens != chunk)
     def _():
@@ -272,10 +275,12 @@
         lax.fori_loop(0, 2, body, 0)
 
     def pair(ref, d):
-        return ref.at[pl.ds((at_x(d) * 2 + core) * 2, 2)]
+        b = at_x(d) * 2 + core
+        return ref.at[b] if ref is tall else ref.at[pl.ds(b * 2, 2)]
 
     def one(ref, d, i):
-        return ref.at[(at_x(d) * 2 + core) * 2 + i]
+        b = (at_x(d) * 2 + core) * 2 + i
+        return wide(ref, b) if ref is tall else ref.at[b]
 
     def x_first(ref):
         mine = pair(ref, 0)
@@ -322,7 +327,7 @@
     def _():
         t_own.wait()
 
-    turn_h = send(tall.at[chunk], tall.at[chunk], mate_h)
+    turn_h = send(wide(tall, chunk), wide(tall, chunk), mate_h)
 
     wait_all(c_core)
     w_copy.wait()
@@ -475,9 +480,9 @@
     wait_all(turn_core)
     wait_all(t_mate)
     total = jnp.zeros((320, 256), F32)
-    for half in range(2):
-        for o in range(NZ):
-            total = total + dot(tall[half * NZ + o], att_all[half, o])
+    for i in range(NZ):
+        half, o = i // 4, i % 4 * 2
+        total = total + dot(tall[i], att_all[half, o : o + 2].reshape(256, 256))
     wg[...] = total
     leaving.append(bring(wg, wg_h))
     wait_exchange(dk_moves)
@@ -523,7 +528,7 @@
         scratch_shapes=[
             *[pltpu.VMEM(kind.shape, kind.dtype) for kind in kinds],
             pltpu.VMEM((2, NZ, 128, 256), BF16),
-            pltpu.VMEM((2 * NZ, 320, HD), BF16),
+            pltpu.VMEM((NZ, 320, 256), BF16),
             pltpu.VMEM((NZ, KV_ROWS, HD), BF16),
             pltpu.VMEM((NZ, 512, HD), BF16),
             pltpu.VMEM((NZ, 256, HD), BF16),

time: 83.3 us -> 83.3 us (level)
  no operation moved by 1% of the time
where the time goes in v4:
time: 83.3 us; the launch traced here: 83.1 us
  Pallas kernels  82.5 us (99%)
    pallas_call x1, Pallas kernels, on_device(): pl.pallas_call(kernel, out_shape=kinds, in_specs=[away] * 8 + [vmem] * 2,...  80.4 us
    pallas_call x1, Pallas kernels, on_device(): pl.pallas_call(finish, out_shape=kinds, in_specs=[away] * 8, out_specs=[a...  2.12 us

profile of v4, /device:TPU:8, one launch (start us, length us, event | category | flops | bytes accessed | tf_op | source)
XLA Modules:
  0.0 83.1 jit_solution(11928398644092477734)
XLA Ops:
  0.6 80.4 %shard_map.161 = (bf16[320,128]{1,0:T(8,128)(2,1)}, bf16[128,256]{1,0:T(8,128)(2,1)}, bf16[128,256]{1,0:T(8,128)(2,1)}, bf16[128,256]{1,0:T(8,128)(2,1)}, bf16[1...) custom-call(bf16[128,256]{1,0:T(8,128)(2,1)} %q.1, ...), custom_call_target="tpu_custom_call" | custom-call | flops 4000000000 | bytes 10000000 | tf_op jit(solution)/shard_map/pallas_call | solution.py:523
  81.0 2.1 %shard_map.162 = (bf16[320,128]{1,0:T(8,128)(2,1)}, bf16[128,256]{1,0:T(8,128)(2,1)}, bf16[128,256]{1,0:T(8,128)(2,1)}, bf16[128,256]{1,0:T(8,128)(2,1)}, bf16[1...) custom-call(bf16[320,128]{1,0:T(8,128)(2,1)} %get-tuple-element.24.refs_0_, ...), custom_call_target="tpu_custom_call" | custom-call | tf_op jit(solution)/shard_map/pallas_call | solution.py:567
